TPU v7x, 32 devices: a whole 2x2x4 slice. The times are simulated.
32 devices in a mesh: wave: 4 (over y, x), slab: 8 (over z, core).
Axes of the slice: x: 2, y: 2, z: 4, core: 2. Of those that a mesh axis runs over, the one named last changes fastest.
Arguments:
- levels: int32 [2048, 2048], P('slab', 'wave'), may hold values from 0 to 15
- offsets: float32 [2048, 2048], P('slab', 'wave'), may hold values from -0.3 to 0.3
- targets: int32 [4, 64, 2], replicated, may hold values from 0 to 2047
- w_in: float32 [256], replicated, may hold values from -96 to 96
- b_in: float32 [256], replicated, may hold values from -87 to 87
- w_out: bfloat16 [256, 8], replicated, may hold values from -0.046875 to 0.046875
- b_out: float32 [8], replicated, may hold values from -2 to 2
Outputs:
- width_gradient: float32 [2048, 2048], P('slab', 'wave')
All inputs are finite; a program needn't handle non-finite values.
Results may differ from a plain program's by a relative error of at most 0.0039.
Values may be sent and summed in bfloat16 or wider, within the bound.
A program may use at most 64 MiB of HBM per device.

v0:
```python
import math

import jax
import jax.numpy as jnp
from jax import lax
from jax.sharding import PartitionSpec as P

LEVELS = 16


def level_widths(levels, offsets):
    return 0.3 + levels.astype(jnp.float32) * (0.4 / (LEVELS - 1)) + offsets


def block_size(rows_count, cols_count):
    size_block = rows_count
    while size_block * cols_count > 32768 and size_block % 2 == 0:
        size_block = size_block // 2
    return size_block


def surrogate_rows(widths, w_in, b_in, w_out, b_out):
    rows_count, cols_count = widths.shape
    size_block = block_size(rows_count, cols_count)
    collected = jnp.zeros((w_out.shape[1], rows_count, cols_count), jnp.bfloat16)

    def surrogate_step_block(turn_index, gathered):
        row_start = turn_index * size_block
        width_piece = lax.dynamic_slice_in_dim(widths, row_start, size_block, 0)
        pre_act = width_piece[..., None] * w_in + b_in
        hidden = (pre_act * jax.nn.sigmoid(pre_act)).astype(jnp.bfloat16)
        mixed_out = (
            jnp.einsum("rch,hj->jrc", hidden, w_out, preferred_element_type=jnp.float32)
            + b_out[:, None, None]
        )
        return lax.dynamic_update_slice_in_dim(
            gathered, mixed_out.astype(jnp.bfloat16), row_start, 1
        )

    return lax.fori_loop(0, rows_count // size_block, surrogate_step_block, collected)


def slope_rows(widths, w_in, b_in, w_out, cotangent):
    rows_count, cols_count = widths.shape
    size_block = block_size(rows_count, cols_count)
    collected = jnp.zeros((rows_count, cols_count), jnp.float32)

    def slope_step_block(turn_index, gathered):
        row_start = turn_index * size_block
        width_piece = lax.dynamic_slice_in_dim(widths, row_start, size_block, 0)
        cot_piece = lax.dynamic_slice_in_dim(cotangent, row_start, size_block, 1)
        pre_act = width_piece[..., None] * w_in + b_in
        sigmoid_value = jax.nn.sigmoid(pre_act)
        back_hidden = jnp.einsum(
            "jrc,hj->rch", cot_piece, w_out, preferred_element_type=jnp.float32
        )
        act_slope = sigmoid_value * (1.0 + pre_act * (1.0 - sigmoid_value))
        rows_out = jnp.sum(back_hidden * act_slope * w_in, axis=-1)
        return lax.dynamic_update_slice_in_dim(gathered, rows_out, row_start, 0)

    return lax.fori_loop(0, rows_count // size_block, slope_step_block, collected)


def frequencies(length, first_index, total_len):
    index_all = first_index + jnp.arange(length, dtype=jnp.int32)
    signed_index = jnp.where(index_all < total_len // 2, index_all, index_all - total_len)
    return signed_index.astype(jnp.float32) * (2.0 * math.pi / total_len)


def transfer(wavelength, kx_rows, ky_cols, focal_length):
    wave_number = 2.0 * math.pi / wavelength
    kz_square = wave_number * wave_number - kx_rows[:, None] ** 2 - ky_cols[None, :] ** 2
    kz_root = jnp.sqrt(jnp.abs(kz_square))
    is_open = kz_square > 0.0
    phase_angle = jnp.where(is_open, focal_length * kz_root, 0.0)
    amplitude = jnp.where(is_open, 1.0, jnp.exp(-focal_length * kz_root))
    return (amplitude * jnp.cos(phase_angle), amplitude * jnp.sin(phase_angle))


def split_factor(length):
    factor = int(math.isqrt(length))
    while length % factor:
        factor = factor - 1
    return factor


def unit_table(rows_count, cols_count, modulus, direction):
    prod_index = (
        jnp.arange(rows_count, dtype=jnp.int32)[:, None]
        * jnp.arange(cols_count, dtype=jnp.int32)[None, :]
        % modulus
    )
    angle_value = prod_index.astype(jnp.float32) * (direction * 2.0 * math.pi / modulus)
    return (jnp.cos(angle_value), jnp.sin(angle_value))


def complex_einsum(spec, left_pair, right_pair):

    def real_dot(first_op, second_op):
        return jnp.einsum(
            spec,
            first_op,
            second_op,
            precision=lax.Precision.HIGHEST,
            preferred_element_type=jnp.float32,
        )

    return (
        real_dot(left_pair[0], right_pair[0]) - real_dot(left_pair[1], right_pair[1]),
        real_dot(left_pair[0], right_pair[1]) + real_dot(left_pair[1], right_pair[0]),
    )


def complex_mul(left_pair, right_pair):
    return (
        left_pair[0] * right_pair[0] - left_pair[1] * right_pair[1],
        left_pair[0] * right_pair[1] + left_pair[1] * right_pair[0],
    )


def transform_last(pair, direction):
    rows_count, length = pair[0].shape
    first_len = split_factor(length)
    second_len = length // first_len
    shaped = (
        pair[0].reshape(rows_count, first_len, second_len),
        pair[1].reshape(rows_count, first_len, second_len),
    )
    section_one = complex_einsum(
        "mab,ak->mkb", shaped, unit_table(first_len, first_len, first_len, direction)
    )
    twiddle = unit_table(first_len, second_len, length, direction)
    turned = complex_mul(section_one, (twiddle[0][None], twiddle[1][None]))
    section_two = complex_einsum(
        "mkb,bl->mlk", turned, unit_table(second_len, second_len, second_len, direction)
    )
    result = (
        section_two[0].reshape(rows_count, length),
        section_two[1].reshape(rows_count, length),
    )
    if direction > 0:
        result = (result[0] / length, result[1] / length)
    return result


def transform_first(pair, direction):
    length, cols_count = pair[0].shape
    first_len = split_factor(length)
    second_len = length // first_len
    shaped = (
        pair[0].reshape(first_len, second_len, cols_count),
        pair[1].reshape(first_len, second_len, cols_count),
    )
    section_one = complex_einsum(
        "abc,ak->kbc", shaped, unit_table(first_len, first_len, first_len, direction)
    )
    twiddle = unit_table(first_len, second_len, length, direction)
    turned = complex_mul(section_one, (twiddle[0][:, :, None], twiddle[1][:, :, None]))
    section_two = complex_einsum(
        "kbc,bl->lkc", turned, unit_table(second_len, second_len, second_len, direction)
    )
    result = (
        section_two[0].reshape(length, cols_count),
        section_two[1].reshape(length, cols_count),
    )
    if direction > 0:
        result = (result[0] / length, result[1] / length)
    return result


def propagate(spectrum_rows, wavelength, focal_length, conjugate):
    column_view = lax.all_to_all(spectrum_rows, "slab", split_axis=2, concat_axis=1, tiled=True)
    length = column_view.shape[1]
    block_cols = column_view.shape[2]
    freq_pair = transform_first((column_view[0], column_view[1]), -1.0)
    kx_all = frequencies(length, 0, length)
    ky_block = frequencies(block_cols, lax.axis_index("slab") * block_cols, length)
    kern_re, kern_im = transfer(wavelength, kx_all, ky_block, focal_length)
    if conjugate:
        kern_im = -kern_im
    filtered = complex_mul(freq_pair, (kern_re, kern_im))
    spatial = transform_first(filtered, 1.0)
    row_view = lax.all_to_all(jnp.stack(spatial), "slab", split_axis=1, concat_axis=2, tiled=True)
    return transform_last((row_view[0], row_view[1]), 1.0)


def local(levels, offsets, targets, w_in, b_in, w_out, b_out):
    rows_here = levels.shape[0]
    wave_count = lax.axis_size("wave")
    length = rows_here * lax.axis_size("slab")
    wave_index = lax.axis_index("wave")
    wavelength = 1.5 + wave_index.astype(jnp.float32) / (wave_count - 1)
    focal_length = float(length // 16)
    widths = level_widths(levels, offsets)
    all_trans = surrogate_rows(widths, w_in, b_in, w_out, b_out).reshape(
        2, wave_count, rows_here, widths.shape[1]
    )
    exchanged = lax.all_to_all(all_trans, "wave", split_axis=1, concat_axis=3, tiled=True)
    spectrum = jnp.stack(
        transform_last(
            (exchanged[0, 0].astype(jnp.float32), exchanged[1, 0].astype(jnp.float32)), -1.0
        )
    )
    field_re, field_im = propagate(spectrum, wavelength, focal_length, False)
    intensity = field_re * field_re + field_im * field_im
    own_targets = lax.dynamic_index_in_dim(targets, wave_index, 0, keepdims=False)
    local_rows = own_targets[:, 0] - lax.axis_index("slab") * rows_here
    inside = (local_rows >= 0) & (local_rows < rows_here)
    spot_map = (
        jnp.zeros((rows_here, length), jnp.float32)
        .at[jnp.clip(local_rows, 0, rows_here - 1), own_targets[:, 1]]
        .add(jnp.where(inside, float(length // 8), 0.0))
    )
    weight = (intensity - spot_map) / wave_count
    adj_spec = jnp.stack(transform_last((weight * field_re, weight * field_im), -1.0))
    back_re, back_im = propagate(adj_spec, wavelength, focal_length, True)
    cotangent = jnp.stack([back_re, back_im]).astype(jnp.bfloat16)
    returned = lax.all_to_all(
        cotangent.reshape(2, 1, rows_here, length), "wave", split_axis=3, concat_axis=1, tiled=True
    )
    return slope_rows(
        widths, w_in, b_in, w_out, returned.reshape(2 * wave_count, rows_here, widths.shape[1])
    )


def solution(mesh):
    placed = (P("slab", "wave"), P("slab", "wave"), P(), P(), P(), P(), P())
    return jax.shard_map(
        local, mesh=mesh, in_specs=placed, out_specs=P("slab", "wave"), check_vma=False
    )
```

profile of v0, /device:TPU:0, one launch (start us, length us, event | category | flops | bytes accessed | tf_op | source)
XLA Modules:
  0.0 952.7 jit_solution(4867431359092800047)
XLA Ops:
  1.6 42.3 %while.26 = (s32[]{:T(128)}, bf16[8,256,512]{2,1,0:T(8,128)(2,1)S(1)}, f32[256,512]{1,0:T(8,128)S(1)}, f32[256]{0:T(256)S(1)}, f32[256]{0:T(256)S(1)}, /*index=5...) while((s32[]{:T(128)}, ...), condition=%wide.region_1.0_spmd, body=%wide.region_0.0_spmd.sunk | while | flops 193462272 | bytes 1972419 | solution.py:40
  1.7 10.3 %fusion.606 = bf16[8,64,512]{2,0,1:T(8,128)(2,1)S(1)} fusion(f32[256]{0:T(256)S(1)} %get-tuple-element.448, f32[256]{0:T(256)S(1)} %get-tuple-element.447, f32[64,512]{1,0:T(8,128)S(1)} %constant_dynamic-slice_fusion.4, f32[8]{0:T(128)S(1)} %get-tuple-element.450, bf16[256,8]{0,1:T(8,128)(2,1)S(1)} %get-tuple-element.449), kind=kOutput, calls=%fused_computation.5.clone.1 | convolution fusion | flops 193462272 | bytes 661536 | tf_op jit(solution)/shard_map/while/body/eval_jaxpr/rch,hj->jrc/dot_general | solution.py:33
  12.2 10.3 %fusion.606 = bf16[8,64,512]{2,0,1:T(8,128)(2,1)S(1)} fusion(f32[256]{0:T(256)S(1)} %get-tuple-element.448, f32[256]{0:T(256)S(1)} %get-tuple-element.447, f32[64,512]{1,0:T(8,128)S(1)} %constant_dynamic-slice_fusion.4, f32[8]{0:T(128)S(1)} %get-tuple-element.450, bf16[256,8]{0,1:T(8,128)(2,1)S(1)} %get-tuple-element.449), kind=kOutput, calls=%fused_computation.5.clone.1 | convolution fusion | flops 193462272 | bytes 661536 | tf_op jit(solution)/shard_map/while/body/eval_jaxpr/rch,hj->jrc/dot_general | solution.py:33
  22.8 10.3 %fusion.606 = bf16[8,64,512]{2,0,1:T(8,128)(2,1)S(1)} fusion(f32[256]{0:T(256)S(1)} %get-tuple-element.448, f32[256]{0:T(256)S(1)} %get-tuple-element.447, f32[64,512]{1,0:T(8,128)S(1)} %constant_dynamic-slice_fusion.4, f32[8]{0:T(128)S(1)} %get-tuple-element.450, bf16[256,8]{0,1:T(8,128)(2,1)S(1)} %get-tuple-element.449), kind=kOutput, calls=%fused_computation.5.clone.1 | convolution fusion | flops 193462272 | bytes 661536 | tf_op jit(solution)/shard_map/while/body/eval_jaxpr/rch,hj->jrc/dot_general | solution.py:33
  33.4 10.3 %fusion.606 = bf16[8,64,512]{2,0,1:T(8,128)(2,1)S(1)} fusion(f32[256]{0:T(256)S(1)} %get-tuple-element.448, f32[256]{0:T(256)S(1)} %get-tuple-element.447, f32[64,512]{1,0:T(8,128)S(1)} %constant_dynamic-slice_fusion.4, f32[8]{0:T(128)S(1)} %get-tuple-element.450, bf16[256,8]{0,1:T(8,128)(2,1)S(1)} %get-tuple-element.449), kind=kOutput, calls=%fused_computation.5.clone.1 | convolution fusion | flops 193462272 | bytes 661536 | tf_op jit(solution)/shard_map/while/body/eval_jaxpr/rch,hj->jrc/dot_general | solution.py:33
  46.3 5.2 all-to-all-start
  51.8 24.5 %all-to-all-done = bf16[2,4,256,512]{2,3,0,1:T(8,128)(2,1)S(1)} async-done(((bf16[2,4,256,512]{2,3,0,1:T(8,128)(2,1)}), bf16[2,4,256,512]{2,3,0,1:T(8,128)(2,1)S(1)}, u32[]{:S(2)}, u32[]{:S(2)}) %all-to-all-start) | async-done | bytes 2097184 | tf_op jit(solution)/shard_map/all_to_all | solution.py:198
  85.9 3.6 fusion.137
  98.4 12.5 %copy.472 = f32[2,256,2048]{1,0,2:T(2,128)} copy(f32[2,256,2048]{1,2,0:T(8,128)S(1)} %pad_maximum_fusion) | data formatting | bytes 8388608 | tf_op jit(solution)/shard_map/stack | solution.py:199
  110.9 5.0 all-to-all-start.1
  116.4 93.7 %all-to-all-done.1 = f32[2,256,2048]{1,0,2:T(2,128)} async-done(((f32[2,256,2048]{1,0,2:T(2,128)}), f32[2,256,2048]{1,0,2:T(2,128)}, u32[]{:S(2)}, u32[]{:S(2)}) %all-to-all-start.1) | async-done | bytes 4194336 | tf_op jit(solution)/shard_map/all_to_all | solution.py:172
  216.9 4.3 fusion.131
  221.3 4.4 fusion.129
  227.8 4.9 fusion.149
  232.7 3.7 multiply_subtract_fusion.3
  239.5 3.5 fusion.121
  247.4 3.2 fusion.158
  251.8 9.4 fusion.21
  270.3 3.9 multiply_subtract_fusion.2
  284.9 3.6 add_multiply_fusion.1
  290.0 12.3 %copy.500 = f32[2,2048,256]{2,0,1:T(2,128)} copy(f32[2,2048,256]{2,1,0:T(8,128)S(1)} %pad_maximum_fusion.1) | data formatting | bytes 8388608 | tf_op jit(solution)/shard_map/stack | solution.py:183
  302.3 4.7 all-to-all-start.2
  307.3 3.8 scatter_fusion
  311.2 89.9 %all-to-all-done.2 = f32[2,2048,256]{2,0,1:T(2,128)} async-done(((f32[2,2048,256]{2,0,1:T(2,128)}), f32[2,2048,256]{2,0,1:T(2,128)}, u32[]{:S(2)}, u32[]{:S(2)}) %all-to-all-start.2) | async-done | bytes 4194336 | tf_op jit(solution)/shard_map/all_to_all | solution.py:183
  407.9 4.3 fusion.99
  412.2 4.4 fusion.97
  419.9 4.9 fusion.171
  424.8 5.7 subtract_bitcast_fusion.3
  433.6 4.4 fusion.91
  443.8 3.4 copy.518
  447.2 4.7 multiply_bitcast_fusion.1
  457.6 5.1 fusion.24
  464.7 4.3 fusion.83
  469.0 4.4 fusion.81
  475.5 4.9 fusion.181
  480.4 3.7 subtract_bitcast_fusion.2
  487.2 3.5 fusion.73
  499.7 10.5 %copy.534 = f32[2,256,2048]{1,0,2:T(2,128)S(1)} copy(f32[2,256,2048]{1,2,0:T(8,128)S(1)} %pad_maximum_fusion.2) | data formatting | bytes 8388608 | tf_op jit(solution)/shard_map/stack | solution.py:215
  510.2 96.5 %all_to_all.90 = f32[2,256,2048]{1,0,2:T(2,128)S(1)} all-to-all(f32[2,256,2048]{1,0,2:T(2,128)S(1)} %copy.534), channel_id=1, replica_groups=mesh['wave'=4,'slab'=8] {'slab'}, dimensions={2} | all-to-all | bytes 8388608 | tf_op jit(solution)/shard_map/all_to_all | solution.py:172
  611.4 4.3 fusion.67
  615.8 4.4 fusion.65
  622.3 4.9 fusion.191
  627.1 3.7 multiply_subtract_fusion.1
  634.0 3.3 fusion.57
  637.3 3.2 fusion.197
  646.1 9.7 %fusion.19 = (f32[32,64,256]{2,1,0:T(8,128)S(1)}, f32[32,64,256]{2,1,0:T(8,128)S(1)}) fusion(f32[256]{0:T(256)S(1)} %fusion.320, f32[32,64]{1,0:T(8,128)S(1)} %fusion.279, f32[32,64,256]{2,1,0:T(8,128)S(1)} %bitcast.313, f32[32,64,256]{2,1,0:T(8,128)S(1)} %bitcast.311), kind=kLoop, calls=%fused_computation.35 | loop fusion | flops 8388608 | bytes 8397824 | tf_op jit(solution)/shard_map/sub | solution.py:116
  664.9 3.9 multiply_subtract_fusion
  679.4 3.4 add_multiply_fusion
  684.3 10.5 %copy.558 = f32[2,2048,256]{2,0,1:T(2,128)S(1)} copy(f32[2,2048,256]{2,1,0:T(8,128)S(1)} %pad_maximum_fusion.3) | data formatting | bytes 8388608 | tf_op jit(solution)/shard_map/stack | solution.py:183
  694.8 96.5 %all_to_all.91 = f32[2,2048,256]{2,0,1:T(2,128)S(1)} all-to-all(f32[2,2048,256]{2,0,1:T(2,128)S(1)} %copy.558), channel_id=1, replica_groups=mesh['wave'=4,'slab'=8] {'slab'}, dimensions={1} | all-to-all | bytes 8388608 | tf_op jit(solution)/shard_map/all_to_all | solution.py:183
  796.0 4.3 fusion.35
  800.3 4.4 fusion.33
  807.1 4.9 fusion.213
  812.0 3.7 subtract_bitcast_fusion
  818.8 3.3 fusion.25
  829.8 14.0 %copy.572 = bf16[2,1,256,2048]{2,0,1,3:T(2,128)(2,1)} copy(bf16[2,1,256,2048]{2,3,1,0:T(8,128)(2,1)S(1)} %pad_maximum_fusion.4) | data formatting | bytes 4194304 | tf_op jit(solution)/shard_map/stack | solution.py:217
  843.8 3.8 all-to-all-start.5
  847.6 24.7 %all-to-all-done.5 = bf16[2,1,256,2048]{2,0,1,3:T(2,128)(2,1)S(1)} async-done(((bf16[2,1,256,2048]{2,0,1,3:T(2,128)(2,1)}), bf16[2,1,256,2048]{2,0,1,3:T(2,128)(2,1)S(1)}, u32[]{:S(2)}, u32[]{:S(2)}) %all-to-all-start.5) | async-done | bytes 2097184 | tf_op jit(solution)/shard_map/all_to_all | solution.py:218
  874.0 3.4 copy.574
  877.5 73.5 %while.27 = (s32[]{:T(128)}, f32[256,512]{1,0:T(8,128)S(1)}, bf16[8,256,512]{2,0,1:T(8,128)(2,1)S(1)}, bf16[256,8]{0,1:T(8,128)(2,1)S(1)}, f32[256,512]{1,0:T(8,...) while((s32[]{:T(128)}, f32[256,512]{1,0:T(8,128)S(1)}, ...), condition=%wide.region_5.6_spmd, body=%wide.region_3.5_spmd.sunk | while | flops 234848256 | bytes 1317031 | solution.py:61
  878.4 17.4 %multiply_reduce_fusion.2 = f32[64,512]{1,0:T(8,128)S(1)} fusion(f32[256]{0:T(256)S(1)} %get-tuple-element.483, f32[256]{0:T(256)S(1)} %get-tuple-element.482, f32[64,512]{1,0:T(8,128)S(1)} %constant_dynamic-slice_fusion.5, bf16[8,256,512]{2,0,1:T(8,128)(2,1)S(1)} %get-tuple-element.479, s32[]{:T(128)S(6)} %select_n.676, ...), kind=kOutput, calls=%fused_computation.10.clone.1 | convolution fusion | flops 234848256 | bytes 792580 | tf_op jit(solution)/shard_map/while/body/eval_jaxpr/jrc,hj->rch/dot_general | solution.py:54
  896.8 17.4 %multiply_reduce_fusion.2 = f32[64,512]{1,0:T(8,128)S(1)} fusion(f32[256]{0:T(256)S(1)} %get-tuple-element.483, f32[256]{0:T(256)S(1)} %get-tuple-element.482, f32[64,512]{1,0:T(8,128)S(1)} %constant_dynamic-slice_fusion.5, bf16[8,256,512]{2,0,1:T(8,128)(2,1)S(1)} %get-tuple-element.479, s32[]{:T(128)S(6)} %select_n.676, ...), kind=kOutput, calls=%fused_computation.10.clone.1 | convolution fusion | flops 234848256 | bytes 792580 | tf_op jit(solution)/shard_map/while/body/eval_jaxpr/jrc,hj->rch/dot_general | solution.py:54
  915.2 17.4 %multiply_reduce_fusion.2 = f32[64,512]{1,0:T(8,128)S(1)} fusion(f32[256]{0:T(256)S(1)} %get-tuple-element.483, f32[256]{0:T(256)S(1)} %get-tuple-element.482, f32[64,512]{1,0:T(8,128)S(1)} %constant_dynamic-slice_fusion.5, bf16[8,256,512]{2,0,1:T(8,128)(2,1)S(1)} %get-tuple-element.479, s32[]{:T(128)S(6)} %select_n.676, ...), kind=kOutput, calls=%fused_computation.10.clone.1 | convolution fusion | flops 234848256 | bytes 792580 | tf_op jit(solution)/shard_map/while/body/eval_jaxpr/jrc,hj->rch/dot_general | solution.py:54
  933.6 17.4 %multiply_reduce_fusion.2 = f32[64,512]{1,0:T(8,128)S(1)} fusion(f32[256]{0:T(256)S(1)} %get-tuple-element.483, f32[256]{0:T(256)S(1)} %get-tuple-element.482, f32[64,512]{1,0:T(8,128)S(1)} %constant_dynamic-slice_fusion.5, bf16[8,256,512]{2,0,1:T(8,128)(2,1)S(1)} %get-tuple-element.479, s32[]{:T(128)S(6)} %select_n.676, ...), kind=kOutput, calls=%fused_computation.10.clone.1 | convolution fusion | flops 234848256 | bytes 792580 | tf_op jit(solution)/shard_map/while/body/eval_jaxpr/jrc,hj->rch/dot_general | solution.py:54
  (146 shorter events, 165.0 us)
Async XLA Ops:
  0.0 307.0 %copy-start = (s32[4,64,2]{1,2,0:T(2,128)S(1)}, s32[4,64,2]{1,2,0:T(2,128)}, u32[]{:S(2)}) copy-start(s32[4,64,2]{1,2,0:T(2,128)} %param.13) | copy-start | bytes 6148
  0.0 1.6 copy-start.14
  0.0 1.6 copy-start.16
  0.0 1.6 copy-start.12
  0.0 1.6 copy-start.18
  43.9 2.4 copy-start.10
  46.3 30.0 %all-to-all-start = ((bf16[2,4,256,512]{2,3,0,1:T(8,128)(2,1)}), bf16[2,4,256,512]{2,3,0,1:T(8,128)(2,1)S(1)}, u32[]{:S(2)}, u32[]{:S(2)}) async-start(bf16[2,4,256,512]{2,3,0,1:T(8,128)(2,1)} %copy.458), calls=%async_computation | async-start | bytes 4194304 | tf_op jit(solution)/shard_map/all_to_all | solution.py:198
  110.9 99.1 %all-to-all-start.1 = ((f32[2,256,2048]{1,0,2:T(2,128)}), f32[2,256,2048]{1,0,2:T(2,128)}, u32[]{:S(2)}, u32[]{:S(2)}) async-start(f32[2,256,2048]{1,0,2:T(2,128)} %copy.472), calls=%async_computation.1 | async-start | bytes 8388608 | tf_op jit(solution)/shard_map/all_to_all | solution.py:172
  227.8 4.9 copy-start.7
  302.3 98.7 %all-to-all-start.2 = ((f32[2,2048,256]{2,0,1:T(2,128)}), f32[2,2048,256]{2,0,1:T(2,128)}, u32[]{:S(2)}, u32[]{:S(2)}) async-start(f32[2,2048,256]{2,0,1:T(2,128)} %copy.500), calls=%async_computation.2 | async-start | bytes 8388608 | tf_op jit(solution)/shard_map/all_to_all | solution.py:183
  311.1 92.4 %copy-start.3 = (f32[256,2048]{1,0:T(8,128)}, f32[256,2048]{1,0:T(8,128)S(1)}, u32[]{:S(2)}) copy-start(f32[256,2048]{1,0:T(8,128)S(1)} %scatter_fusion) | copy-start | bytes 6291460
  418.6 1.4 copy-start.2
  419.9 4.9 copy-start.8
  454.5 3.1 copy-start.4
  475.5 4.9 copy-start.9
  622.2 4.9 copy-start.5
  807.1 4.9 copy-start.6
  843.8 28.6 %all-to-all-start.5 = ((bf16[2,1,256,2048]{2,0,1,3:T(2,128)(2,1)}), bf16[2,1,256,2048]{2,0,1,3:T(2,128)(2,1)S(1)}, u32[]{:S(2)}, u32[]{:S(2)}) async-start(bf16[2,1,256,2048]{2,0,1,3:T(2,128)(2,1)} %copy.572), calls=%async_computation.5 | async-start | bytes 4194304 | tf_op jit(solution)/shard_map/all_to_all | solution.py:218
  874.0 3.5 copy-start.13
  874.0 3.5 copy-start.15
  874.0 3.5 copy-start.17
  951.0 0.8 copy-start.11
  951.8 0.7 copy-start.1
where the time goes:
time: 964 us; the launch traced here: 953 us
  matrix products  337 us (35%)
  waiting for transfers between devices  233 us (24%)
  blocking collectives  193 us (20%)
  local copies, waits for them, and re-layouts  139 us (14%)
  other arithmetic  31 us (3%)
  starting transfers between devices  18.7 us (2%)
    dot_general x64, matrix products, real_dot(): jnp.einsum(spec, first_op, second_op, precision=lax.Precision.HIGHEST, pr...  226 us
    all_to_all x1, blocking collectives, propagate(): lax.all_to_all(spectrum_rows, 'slab', split_axis=2, concat_axis=1, tiled=...  96.5 us
    all_to_all x1, blocking collectives, propagate(): lax.all_to_all(jnp.stack(spatial), 'slab', split_axis=1, concat_axis=2, t...  96.5 us
    all_to_all x1, waiting for transfers between devices, propagate(): lax.all_to_all(spectrum_rows, 'slab', split_axis=2, concat_axis=1, tiled=...  93.7 us
    all_to_all x1, waiting for transfers between devices, propagate(): lax.all_to_all(jnp.stack(spatial), 'slab', split_axis=1, concat_axis=2, t...  89.9 us
    dot_general x4, matrix products, slope_step_block(): jnp.einsum('jrc,hj->rch', cot_piece, w_out, preferred_element_type=jnp.fl...  69.6 us
    dot_general x4, matrix products, surrogate_step_block(): jnp.einsum('rch,hj->jrc', hidden, w_out, preferred_element_type=jnp.float32)  41.3 us
    all_to_all x1, waiting for transfers between devices, local(): lax.all_to_all(cotangent.reshape(2, 1, rows_here, length), 'wave', split_...  24.7 us
  transfers between devices with their start and end apart: 4, of which 4 were waited for; matrix products, arithmetic and copies ran while one was open for 0% of the time, Pallas kernels for 0%

commit v1 on v0

v1 whole, which is shorter than its diff:
```python
import math

import jax
import jax.numpy as jnp
import ml_dtypes
import numpy as np
from jax import lax
from jax.experimental import pallas as pl
from jax.experimental.pallas import tpu as pltpu
from jax.sharding import Mesh, PartitionSpec as P

LEVELS = 16
RADIX = 8
ROWS = 16
GRANT = 58 * 1024 * 1024
GROUP = ("wave", "duo")
SLAB = ("zed", "duo")


def params(**more):
    return pltpu.CompilerParams(vmem_limit_bytes=GRANT, **more)


def split16(table):
    high = table.astype(np.float32).astype(ml_dtypes.bfloat16)
    low = (table - high.astype(np.float64)).astype(np.float32).astype(ml_dtypes.bfloat16)
    return high, low


def dft_block(points):
    index = np.arange(points)
    angle = -2.0 * np.pi * ((index[:, None] * index[None, :]) % points) / points
    re, im = np.cos(angle), np.sin(angle)
    return split16(np.block([[re, -im], [im, re]]))


def twiddles(points):
    angle = -2.0 * np.pi * np.outer(np.arange(RADIX), np.arange(points)) / (RADIX * points)
    return np.stack([np.cos(angle), np.sin(angle)]).astype(np.float32)


def add(a, b):
    return (a[0] + b[0], a[1] + b[1])


def sub(a, b):
    return (a[0] - b[0], a[1] - b[1])


def turn(a, sign):
    return (-a[1], a[0]) if sign > 0 else (a[1], -a[0])


def dft4(x, sign):
    a, b = add(x[0], x[2]), sub(x[0], x[2])
    c, d = add(x[1], x[3]), turn(sub(x[1], x[3]), sign)
    return [add(a, c), add(b, d), sub(a, c), sub(b, d)]


def dft8(x, sign):
    even, odd = dft4(x[0::2], sign), dft4(x[1::2], sign)
    half = math.sqrt(0.5)
    one = add(odd[1], turn(odd[1], sign))
    three = sub(turn(odd[3], sign), odd[3])
    odd = [odd[0], (one[0] * half, one[1] * half), turn(odd[2], sign), (three[0] * half, three[1] * half)]
    return [add(e, o) for e, o in zip(even, odd)] + [sub(e, o) for e, o in zip(even, odd)]


def mul(a, b):
    return (a[0] * b[0] - a[1] * b[1], a[0] * b[1] + a[1] * b[0])


def mul_conj(a, b):
    return (a[0] * b[0] + a[1] * b[1], a[1] * b[0] - a[0] * b[1])


def dot(a, b):
    return jnp.dot(a, b, preferred_element_type=jnp.float32)


def halves(x):
    high = x.astype(jnp.bfloat16)
    return high, (x - high.astype(jnp.float32)).astype(jnp.bfloat16)


FULL = 32000.0
LOG2 = math.log(2.0)


def send_rows(rows, coded):
    return 2 * rows + (ROWS if coded else 0)


def put_block(out_ref, k, y):
    rows, lanes = y.shape
    if out_ref.dtype != jnp.int16:
        out_ref[k] = y
        return
    largest = jnp.maximum(jnp.max(jnp.abs(y), axis=0, keepdims=True), 1e-30)
    power = jnp.ceil(jnp.log(largest) * (1.0 / LOG2) + 0.001)
    factor = FULL / jnp.exp(power * LOG2)
    out_ref[k, :rows] = jnp.round(y * factor).astype(jnp.int32).astype(jnp.int16)
    out_ref[k, rows:] = jnp.broadcast_to(power, (ROWS, lanes)).astype(jnp.int32).astype(jnp.int16)


def block_scale(in_ref, k):
    if in_ref.dtype != jnp.int16:
        return None
    power = in_ref[k, in_ref.shape[1] - ROWS :].astype(jnp.int32).astype(jnp.float32)
    return jnp.exp(power * LOG2) * (1.0 / FULL)


def as_float(x):
    return x.astype(jnp.int32).astype(jnp.float32) if x.dtype == jnp.int16 else x


def width_of(levels_ref, offsets_ref):
    return 0.3 + levels_ref[...].astype(jnp.float32) * (0.4 / (LEVELS - 1)) + offsets_ref[...]


def surrogate_kernel(levels_ref, offsets_ref, slope_ref, bias_ref, out_w_ref, out_b_ref, t_ref, width_s, mix_s):
    waves, duo, parts, rows, cols = t_ref.shape
    width_s[...] = width_of(levels_ref, offsets_ref)
    units = slope_ref.shape[0]
    lane = slope_ref.shape[1]
    count = width_s.shape[1] // lane
    for r in range(rows):
        for c in range(count):
            w = jnp.broadcast_to(width_s[r : r + 1, c * lane : (c + 1) * lane], (units, lane))
            y = w * slope_ref[...] + bias_ref[...]
            hidden = (y * jnp.tanh(y) + y).astype(jnp.bfloat16)
            mixed = dot(out_w_ref[...], hidden)[: waves * parts] + out_b_ref[...]
            mix_s[:, r, c * lane : (c + 1) * lane] = mixed
    for wave in range(waves):
        for d in range(duo):
            for part in range(parts):
                t_ref[wave, d, part] = mix_s[wave * parts + part, :, d * cols : (d + 1) * cols].astype(jnp.bfloat16)


def slope_kernel(levels_ref, offsets_ref, slope_ref, bias_ref, back_w_ref, cot_ref, grad_ref, width_s, mix_s):
    waves, duo, parts, rows, cols = cot_ref.shape
    width_s[...] = width_of(levels_ref, offsets_ref)
    units = slope_ref.shape[0]
    lane = slope_ref.shape[1]
    count = width_s.shape[1] // lane
    js = waves * parts
    for r in range(rows):
        for c in range(count):
            w = jnp.broadcast_to(width_s[r : r + 1, c * lane : (c + 1) * lane], (units, lane))
            y = w * slope_ref[...] + bias_ref[...]
            th = jnp.tanh(y)
            act = ((1.0 + th) * (1.0 + (y - y * th))).astype(jnp.bfloat16)
            mixed = dot(back_w_ref[...], act)
            mix_s[:, r, c * lane : (c + 1) * lane] = mixed[:js] + mixed[js : 2 * js]
    for d in range(duo):
        at = slice(d * cols, (d + 1) * cols)
        total = jnp.zeros((rows, cols), jnp.float32)
        for wave in range(waves):
            for part in range(parts):
                total = total + mix_s[wave * parts + part, :, at] * cot_ref[wave, d, part].astype(jnp.float32)
        grad_ref[:, at] = total


def unit_tables(w_in, b_in, lane):
    units = w_in.shape[0]
    spread = lambda x: jnp.broadcast_to((0.5 * x)[:, None], (units, lane))
    return spread(w_in), spread(b_in)


def whole(shape):
    return pl.BlockSpec(shape, lambda i: (0,) * len(shape))


def surrogate(levels, offsets, w_in, b_in, w_out, b_out, waves, duo):
    rows, cols = levels.shape
    parts = 2
    js = waves * parts
    units = w_in.shape[0]
    lane = min(256, cols)
    slope, bias = unit_tables(w_in, b_in, lane)
    ordered = w_out.reshape(units, parts, waves).transpose(2, 1, 0).reshape(js, units)
    pad = max(16, js)
    ordered = jnp.zeros((pad, units), jnp.bfloat16).at[:js].set(ordered)
    biases = b_out.reshape(parts, waves).T.reshape(js, 1)
    shape = (waves, duo, parts, rows, cols // duo)
    strip = pl.BlockSpec((ROWS, cols), lambda i: (i, 0))
    return pl.pallas_call(
        surrogate_kernel,
        grid=(rows // ROWS,),
        in_specs=[strip, strip, whole(slope.shape), whole(bias.shape), whole(ordered.shape), whole(biases.shape)],
        out_specs=pl.BlockSpec(shape[:3] + (ROWS, cols // duo), lambda i: (0, 0, 0, i, 0)),
        out_shape=jax.ShapeDtypeStruct(shape, jnp.bfloat16),
        scratch_shapes=[pltpu.VMEM((ROWS, cols), jnp.float32), pltpu.VMEM((js, ROWS, cols), jnp.float32)],
        compiler_params=params(),
        name="surrogate",
    )(levels, offsets, slope, bias, ordered, biases)


def width_slope(levels, offsets, w_in, b_in, w_out, cot):
    rows, cols = levels.shape
    waves, duo, parts = cot.shape[:3]
    js = waves * parts
    units = w_in.shape[0]
    lane = min(256, cols)
    slope, bias = unit_tables(w_in, b_in, lane)
    ordered = w_out.astype(jnp.float32).reshape(units, parts, waves).transpose(2, 1, 0).reshape(js, units)
    high, low = halves(ordered * (0.5 * w_in)[None, :])
    weights = jnp.concatenate([high, low])
    strip = pl.BlockSpec((ROWS, cols), lambda i: (i, 0))
    return pl.pallas_call(
        slope_kernel,
        grid=(rows // ROWS,),
        in_specs=[
            strip,
            strip,
            whole(slope.shape),
            whole(bias.shape),
            whole(weights.shape),
            pl.BlockSpec(cot.shape[:3] + (ROWS, cols // duo), lambda i: (0, 0, 0, i, 0)),
        ],
        out_specs=strip,
        out_shape=jax.ShapeDtypeStruct((rows, cols), jnp.float32),
        scratch_shapes=[pltpu.VMEM((ROWS, cols), jnp.float32), pltpu.VMEM((js, ROWS, cols), jnp.float32)],
        compiler_params=params(),
        name="width_slope",
    )(levels, offsets, slope, bias, weights, cot)


def col_forward_chunks(load, tw_ref, hi_s, lo_s):
    points, cols = hi_s.shape[1] // 2, hi_s.shape[2]
    lane = tw_ref.shape[3]

    def chunk(i, _):
        row = pl.multiple_of(i * ROWS, ROWS)
        at = pl.ds(row, ROWS)
        at_im = pl.ds(pl.multiple_of(points + row, ROWS), ROWS)
        for c in range(cols // lane):
            lanes = slice(c * lane, (c + 1) * lane)
            out = dft8([load(n, at, lanes) for n in range(RADIX)], -1)
            for k in range(RADIX):
                pair = out[k] if k == 0 else mul(out[k], (tw_ref[0, k, at, :], tw_ref[1, k, at, :]))
                hi_s[k, at, lanes], lo_s[k, at, lanes] = halves(pair[0])
                hi_s[k, at_im, lanes], lo_s[k, at_im, lanes] = halves(pair[1])
        return 0

    lax.fori_loop(0, points // ROWS, chunk, 0)


def col_forward_dots(fh_ref, fl_ref, hi_s, lo_s, out_ref):
    points = hi_s.shape[1] // 2

    def step(k, _):
        high = hi_s[k]
        y = dot(fh_ref[...], high) + dot(fh_ref[...], lo_s[k]) + dot(fl_ref[...], high)
        put_block(out_ref, k, y)
        return 0

    lax.fori_loop(0, RADIX, step, 0)


def col_inverse_dots(in_ref, gh_ref, gl_ref, tw_ref, mid_s):
    points, cols = mid_s.shape[2], mid_s.shape[3]
    lane = tw_ref.shape[3]
    scale = 1.0 / (RADIX * points)

    def step(k, _):
        high, low = halves(as_float(in_ref[k, : 2 * points]))
        z = dot(gh_ref[...], high) + dot(gh_ref[...], low) + dot(gl_ref[...], high)
        sent = block_scale(in_ref, k)
        z = z * (scale if sent is None else sent[:1] * scale)
        for c in range(cols // lane):
            lanes = slice(c * lane, (c + 1) * lane)
            pair = mul_conj((z[:points, lanes], z[points:, lanes]), (tw_ref[0, k], tw_ref[1, k]))
            mid_s[k, 0, :, lanes] = pair[0]
            mid_s[k, 1, :, lanes] = pair[1]
        return 0

    lax.fori_loop(0, RADIX, step, 0)


def first_kernel(t_ref, tw_ref, fh_ref, fl_ref, out_ref, hi_s, lo_s):
    def load(n, at, lanes):
        return (t_ref[n, 0, at, lanes].astype(jnp.float32), t_ref[n, 1, at, lanes].astype(jnp.float32))

    col_forward_chunks(load, tw_ref, hi_s, lo_s)
    col_forward_dots(fh_ref, fl_ref, hi_s, lo_s, out_ref)


def focus_kernel(level, waves, in_ref, tw_ref, fh_ref, fl_ref, gh_ref, gl_ref, rowsel_ref, colsel_ref, out_ref, hi_s, lo_s, mid_s, spot_s):
    points, cols = mid_s.shape[2], mid_s.shape[3]
    lane = tw_ref.shape[3]
    col_inverse_dots(in_ref, gh_ref, gl_ref, tw_ref, mid_s)
    for n in range(RADIX):
        spot_s[n] = dot(rowsel_ref[n], colsel_ref[...]) * level

    def chunk(i, _):
        at = pl.ds(pl.multiple_of(i * ROWS, ROWS), ROWS)
        for c in range(cols // lane):
            lanes = slice(c * lane, (c + 1) * lane)
            out = dft8([(mid_s[k, 0, at, lanes], mid_s[k, 1, at, lanes]) for k in range(RADIX)], 1)
            for n in range(RADIX):
                re, im = out[n]
                weight = (re * re + im * im - spot_s[n, at, lanes]) * (1.0 / waves)
                mid_s[n, 0, at, lanes] = weight * re
                mid_s[n, 1, at, lanes] = weight * im
        return 0

    lax.fori_loop(0, points // ROWS, chunk, 0)

    def load(n, at, lanes):
        return (mid_s[n, 0, at, lanes], mid_s[n, 1, at, lanes])

    col_forward_chunks(load, tw_ref, hi_s, lo_s)
    col_forward_dots(fh_ref, fl_ref, hi_s, lo_s, out_ref)


def last_kernel(in_ref, tw_ref, gh_ref, gl_ref, out_ref, mid_s):
    points, cols = mid_s.shape[2], mid_s.shape[3]
    lane = tw_ref.shape[3]
    col_inverse_dots(in_ref, gh_ref, gl_ref, tw_ref, mid_s)

    def chunk(i, _):
        at = pl.ds(pl.multiple_of(i * ROWS, ROWS), ROWS)
        for c in range(cols // lane):
            lanes = slice(c * lane, (c + 1) * lane)
            out = dft8([(mid_s[k, 0, at, lanes], mid_s[k, 1, at, lanes]) for k in range(RADIX)], 1)
            for n in range(RADIX):
                out_ref[n, 0, at, lanes] = out[n][0].astype(jnp.bfloat16)
                out_ref[n, 1, at, lanes] = out[n][1].astype(jnp.bfloat16)
        return 0

    lax.fori_loop(0, points // ROWS, chunk, 0)


def filter_kernel(conjugate, in_ref, kern_ref, tw_ref, fh_ref, fl_ref, gh_ref, gl_ref, out_ref, hi_s, lo_s, mid_s, sent_s):
    rows, points = mid_s.shape[2], mid_s.shape[3]
    lane = 128
    scale = 1.0 / (RADIX * points)
    coded = in_ref.dtype == jnp.int16
    if coded:
        for n in range(RADIX):
            sent_s[n] = block_scale(in_ref, n)

    def load(n, at, lanes):
        x = as_float(in_ref[n, at, lanes])
        return x * sent_s[n, :, lanes] if coded else x

    def forward(i, _):
        at = pl.ds(pl.multiple_of(i * ROWS, ROWS), ROWS)
        at_im = pl.ds(pl.multiple_of(rows + i * ROWS, ROWS), ROWS)
        for c in range(points // lane):
            lanes = slice(c * lane, (c + 1) * lane)
            lanes_im = slice(points + c * lane, points + (c + 1) * lane)
            out = dft8([(load(n, at, lanes), load(n, at_im, lanes)) for n in range(RADIX)], -1)
            for k in range(RADIX):
                pair = out[k] if k == 0 else mul(out[k], (tw_ref[0, k, :, lanes], tw_ref[1, k, :, lanes]))
                hi_s[k, at, lanes], lo_s[k, at, lanes] = halves(pair[0])
                hi_s[k, at, lanes_im], lo_s[k, at, lanes_im] = halves(pair[1])
        return 0

    lax.fori_loop(0, rows // ROWS, forward, 0)
    combine = mul_conj if conjugate else mul

    def step(k, _):
        high = hi_s[k]
        y = dot(high, gh_ref[...]) + dot(lo_s[k], gh_ref[...]) + dot(high, gl_ref[...])
        re, im = combine((y[:, :points], y[:, points:]), (kern_ref[0, k], kern_ref[1, k]))
        re_h, re_l = halves(re)
        im_h, im_l = halves(im)
        high = jnp.concatenate([re_h, im_h], axis=1)
        low = jnp.concatenate([re_l, im_l], axis=1)
        z = dot(high, fh_ref[...]) + dot(low, fh_ref[...]) + dot(high, fl_ref[...])
        z = z * scale
        t_re, t_im = tw_ref[0, k, 0:1, :], tw_ref[1, k, 0:1, :]
        pair = mul_conj((z[:, :points], z[:, points:]), (t_re, t_im))
        mid_s[k, 0] = pair[0]
        mid_s[k, 1] = pair[1]
        return 0

    lax.fori_loop(0, RADIX, step, 0)

    def inverse(i, _):
        at = pl.ds(pl.multiple_of(i * ROWS, ROWS), ROWS)
        for c in range(points // lane):
            lanes = slice(c * lane, (c + 1) * lane)
            out = dft8([(mid_s[k, 0, at, lanes], mid_s[k, 1, at, lanes]) for k in range(RADIX)], 1)
            for n in range(RADIX):
                mid_s[n, 0, at, lanes], mid_s[n, 1, at, lanes] = out[n]
        return 0

    lax.fori_loop(0, rows // ROWS, inverse, 0)

    def send(n, _):
        put_block(out_ref, n, mid_s[n].reshape(2 * rows, points))
        return 0

    lax.fori_loop(0, RADIX, send, 0)


def call(kernel, out_shape, out_type, scratch, name, *args):
    return pl.pallas_call(
        kernel,
        out_shape=jax.ShapeDtypeStruct(out_shape, out_type),
        scratch_shapes=scratch,
        compiler_params=params(),
        name=name,
    )(*args)


def frequencies(index_all, total_len):
    signed_index = jnp.where(index_all < total_len // 2, index_all, index_all - total_len)
    return signed_index.astype(jnp.float32) * (2.0 * math.pi / total_len)


def transfer(wavelength, kx, ky, focal_length):
    wave_number = 2.0 * math.pi / wavelength
    kz_square = wave_number * wave_number - kx**2 - ky**2
    kz_root = jnp.sqrt(jnp.abs(kz_square))
    is_open = kz_square > 0.0
    phase_angle = jnp.where(is_open, focal_length * kz_root, 0.0)
    amplitude = jnp.where(is_open, 1.0, jnp.exp(-focal_length * kz_root))
    return jnp.stack([amplitude * jnp.cos(phase_angle), amplitude * jnp.sin(phase_angle)])


def local(levels, offsets, targets, w_in, b_in, w_out, b_out):
    waves, duo = lax.axis_size("wave"), lax.axis_size("duo")
    slabs, group = waves * duo, waves * duo
    rows_here, cols_here = levels.shape
    length = rows_here * slabs
    points = length // RADIX
    cols = cols_here // duo
    rows = length // group
    own = lax.axis_index("wave") * duo + lax.axis_index("duo")
    wave_index = lax.axis_index("zed")
    wavelength = 1.5 + wave_index.astype(jnp.float32) / (waves - 1)

    def exchange(x, axes):
        return lax.all_to_all(x, axes, split_axis=0, concat_axis=0, tiled=True)

    def regroup(x, blocks):
        if x.shape[0] == blocks:
            return x
        flat = x.transpose(1, 0, 2, 3).reshape(2, blocks, -1, x.shape[3])
        return flat.transpose(1, 0, 2, 3)

    def recolumn(x, blocks):
        if x.shape[0] == blocks:
            return x
        flat = x.transpose(1, 2, 0, 3).reshape(2, x.shape[2], blocks, -1)
        return flat.transpose(2, 0, 1, 3)

    fh, fl = dft_block(points)
    gh, gl = fh.T, fl.T
    fh, fl, gh, gl = (jnp.asarray(np.ascontiguousarray(m)) for m in (fh, fl, gh, gl))
    tw = twiddles(points)
    lane = min(128, cols)
    tw_col = jnp.broadcast_to(jnp.asarray(tw)[:, :, :, None], (2, RADIX, points, lane))
    tw_row = jnp.broadcast_to(jnp.asarray(tw)[:, :, None, :], (2, RADIX, ROWS, points))

    position = own * rows + jnp.arange(rows, dtype=jnp.int32)
    u = position // points + RADIX * (position % points)
    v = jnp.arange(RADIX, dtype=jnp.int32)[:, None] + RADIX * jnp.arange(points, dtype=jnp.int32)[None, :]
    kern = transfer(
        wavelength, frequencies(u, length)[None, :, None], frequencies(v, length)[:, None, :], float(length // 16)
    )

    own_targets = lax.dynamic_index_in_dim(targets, wave_index, 0, keepdims=False)
    rowsel = (jnp.arange(length, dtype=jnp.int32)[:, None] == own_targets[None, :, 0]).astype(jnp.bfloat16)
    rowsel = rowsel.reshape(RADIX, points, -1)
    colsel = (own_targets[:, 1:2] - own * cols == jnp.arange(cols, dtype=jnp.int32)[None, :]).astype(jnp.bfloat16)

    col_shape = (RADIX, 2, points, cols)
    row_shape = (RADIX, 2, rows, points)
    col_pair = [pltpu.VMEM((RADIX, 2 * points, cols), jnp.bfloat16)] * 2
    row_pair = [pltpu.VMEM((RADIX, rows, 2 * points), jnp.bfloat16)] * 2
    coded = group == RADIX
    wire = jnp.int16 if coded else jnp.float32
    col_send = (RADIX, send_rows(points, coded), cols)
    row_send = (RADIX, send_rows(rows, coded), points)

    def to_rows(x):
        if coded:
            return exchange(x, GROUP)
        return recolumn(exchange(regroup(x.reshape(col_shape), group), GROUP), RADIX).reshape(row_send)

    def to_cols(x):
        if coded:
            return exchange(x, GROUP)
        return regroup(exchange(recolumn(x.reshape(row_shape), group), GROUP), RADIX).reshape(col_send)

    def filtered(spectrum, conjugate):
        done = call(
            lambda *refs: filter_kernel(conjugate, *refs),
            row_send,
            wire,
            row_pair + [pltpu.VMEM(row_shape, jnp.float32), pltpu.VMEM((RADIX, ROWS, points), jnp.float32)],
            "filter_back" if conjugate else "filter",
            to_rows(spectrum), kern, tw_row, fh, fl, gh, gl,
        )
        return to_cols(done)

    trans = surrogate(levels, offsets, w_in, b_in, w_out, b_out, waves, duo)
    trans = exchange(trans.reshape((slabs,) + trans.shape[2:]), SLAB)
    spectrum = call(first_kernel, col_send, wire, col_pair, "first", regroup(trans, RADIX), tw_col, fh, fl)
    spectrum = filtered(spectrum, False)
    spectrum = call(
        lambda *refs: focus_kernel(float(length // 8), waves, *refs),
        col_send,
        wire,
        col_pair + [pltpu.VMEM(col_shape, jnp.float32), pltpu.VMEM((RADIX, points, cols), jnp.float32)],
        "focus",
        spectrum, tw_col, fh, fl, gh, gl, rowsel, colsel,
    )
    spectrum = filtered(spectrum, True)
    mid = [pltpu.VMEM(col_shape, jnp.float32)]
    cot = call(last_kernel, col_shape, jnp.bfloat16, mid, "last", spectrum, tw_col, gh, gl)
    cot = exchange(regroup(cot, slabs), SLAB)
    return width_slope(levels, offsets, w_in, b_in, w_out, cot.reshape((waves, duo) + cot.shape[1:]))


def solution(mesh):
    waves, slabs = mesh.shape["wave"], mesh.shape["slab"]
    cut = Mesh(mesh.devices.reshape(waves, waves, slabs // waves), ("wave", "zed", "duo"))
    place = P(("zed", "duo"), "wave")
    placed = (place, place, P(), P(), P(), P(), P())
    return jax.shard_map(local, mesh=cut, in_specs=placed, out_specs=place, check_vma=False)
```

time: 964 us -> 392 us (0.41); the launches traced: 953 us -> 392 us
  matrix products: 337 us -> 0 us
  Pallas kernels: 0 us -> 146 us
  waiting for transfers between devices: 233 us -> 89.9 us
  local copies, waits for them, and re-layouts: 139 us -> 10.6 us
  blocking collectives: 193 us -> 119 us
  other arithmetic: 31 us -> 14.7 us
    dot_general x72 -> x0, matrix products: 337 us -> none  [the longest x64 226 us: real_dot(): jnp.einsum(spec, first_op, second_op, precision=lax.Precision.HIGHEST, pr...]
    pallas_call x0 -> x7, Pallas kernels: none -> 146 us  [the longest x5 73.4 us: call(): pl.pallas_call(kernel, out_shape=jax.ShapeDtypeStruct(out_shape, out_type...]
    all_to_all x4 -> x3, waiting for transfers between devices: 233 us -> 89.9 us  [exchange(): return lax.all_to_all(x, axes, split_axis=0, concat_axis=0, tiled=True)]
    all_to_all x2 -> x3, blocking collectives: 193 us -> 119 us  [exchange(): return lax.all_to_all(x, axes, split_axis=0, concat_axis=0, tiled=True)]
    another operation x5 -> x0, local copies, waits for them, and re-layouts: 59.8 us -> none  [the longest x2 22.8 us: propagate(): jnp.stack(spatial)]
    slice x13 -> x0, local copies, waits for them, and re-layouts: 25.9 us -> none  [the longest x6 12.9 us: propagate(): return transform_last((row_view[0], row_view[1]), 1.0)]
    sub x3 -> x1, other arithmetic: 19.1 us -> 0.02 us  [transfer(): kz_square = wave_number * wave_number - kx ** 2 - ky ** 2]
    div x10 -> x0, local copies, waits for them, and re-layouts: 17.7 us -> none  [the longest x6 12.8 us: transform_last(): result = (result[0] / length, result[1] / length)]
  transfers between devices with their start and end apart: 4 -> 3, of which waited for: 4 -> 3; matrix products, arithmetic and copies ran while one was open for 0% -> 3% of each run, Pallas kernels for 0% -> 0%
where the time goes in v1:
time: 392 us
  Pallas kernels  146 us (37%)
  blocking collectives  119 us (30%)
  waiting for transfers between devices  89.9 us (23%)
  other arithmetic  14.7 us (4%)
  starting transfers between devices  11.2 us (3%)
  local copies, waits for them, and re-layouts  10.6 us (3%)
    all_to_all x3, blocking collectives, exchange(): return lax.all_to_all(x, axes, split_axis=0, concat_axis=0, tiled=True)  119 us
    all_to_all x3, waiting for transfers between devices, exchange(): return lax.all_to_all(x, axes, split_axis=0, concat_axis=0, tiled=True)  89.9 us
    pallas_call x5, Pallas kernels, call(): pl.pallas_call(kernel, out_shape=jax.ShapeDtypeStruct(out_shape, out_type...  73.4 us
    pallas_call x1, Pallas kernels, width_slope(): pl.pallas_call(slope_kernel, grid=(rows // ROWS,), in_specs=[strip, strip...  43 us
    pallas_call x1, Pallas kernels, surrogate(): pl.pallas_call(surrogate_kernel, grid=(rows // ROWS,), in_specs=[strip, s...  29.7 us
    all_to_all x3, starting transfers between devices, exchange(): return lax.all_to_all(x, axes, split_axis=0, concat_axis=0, tiled=True)  11.2 us
    mul x1, other arithmetic, transfer(): amplitude * jnp.cos(phase_angle)  8.45 us
  transfers between devices with their start and end apart: 3, of which 3 were waited for; matrix products, arithmetic and copies ran while one was open for 3% of the time, Pallas kernels for 0%

profile of v1, /device:TPU:0, one launch (start us, length us, event | category | flops | bytes accessed | tf_op | source)
XLA Modules:
  0.0 391.6 jit_solution(3670514466043701996)
XLA Ops:
  0.0 0.0 copy-start
  0.0 0.7 broadcast_multiply_fusion.1
  0.7 0.7 broadcast_multiply_fusion
  1.4 0.7 reshape.180
  2.1 0.7 reshape.183
  2.8 0.1 copy.17
  2.9 0.7 reshape.187.out_b_ref
  3.6 0.6 scatter.4.out_w_ref
  4.2 0.8 broadcast_in_dim.12.slope_ref
  5.0 0.8 broadcast_in_dim.13.bias_ref
  5.8 29.7 %surrogate.1 = bf16[4,2,2,256,256]{4,3,2,1,0:T(8,128)(2,1)} custom-call(s32[256,512]{1,0:T(8,128)} %levels_ref.3, f32[256,512]{1,0:T(8,128)} %offsets_ref.3, f32[256,256]{1,0:T(8,128)} %broadcast_in_dim.12.slope_ref, f32[256,256]{1,0:T(8,128)} %broadcast_in_dim.13.bias_ref, bf16[16,256]{1,0:T(8,128)(2,1)} %scatter.4.out_w_ref, f32[8,1]{1,0:T(8,128)} %reshape.187.out_b_ref), custom_call_target="tpu_custom_call" | custom-call | tf_op jit(solution)/shard_map/surrogate/pallas_call | solution.py:187
  35.5 0.0 copy-start.4
  35.5 55.6 %all_to_all.30.t_ref = bf16[8,2,256,256]{3,2,1,0:T(8,128)(2,1)} all-to-all(bf16[8,2,256,256]{3,2,1,0:T(8,128)(2,1)} %bitcast.15), channel_id=1, replica_groups=mesh['wave'=4,'zed'=4,'duo'=2] {'zed','duo'}, dimensions={0} | all-to-all | bytes 4194304 | tf_op jit(solution)/shard_map/all_to_all | solution.py:438
  91.2 0.0 copy-done.4
  91.2 2.0 broadcast_in_dim.15.tw_ref.refs_1_
  93.2 11.1 %first.1 = s16[8,528,256]{2,1,0:T(8,128)(2,1)} custom-call(bf16[8,2,256,256]{3,2,1,0:T(8,128)(2,1)} %all_to_all.30.t_ref, f32[2,8,256,128]{3,2,1,0:T(8,128)} %broadcast_in_dim.15.tw_ref.refs_1_, bf16[512,512]{1,0:T(8,128)(2,1)} %constant.116.clone.fh_ref.refs_3_.refs_2_, bf16[512,512]{1,0:T(8,128)(2,1)} %constant.117.clone.fl_ref.refs_4_.refs_3_), custom_call_target="tpu_custom_call" | custom-call | tf_op jit(solution)/shard_map/first/pallas_call | solution.py:401
  104.3 3.8 all-to-all-start.1
  108.2 8.4 %fusion.7 = (f32[1,8,256,256]{3,2,1,0:T(8,128)S(1)}, f32[1,8,256,256]{3,2,1,0:T(8,128)S(1)}) fusion(f32[8,256]{1,0:T(8,128)S(1)} %fusion.13, f32[256]{0:T(256)S(1)} %fusion.20), kind=kLoop, calls=%fused_computation.10 | loop fusion | flops 4718592 | bytes 4203520 | tf_op jit(solution)/shard_map/mul | solution.py:422
  116.6 2.4 pad_maximum_fusion.refs_1_
  119.0 16.4 %all-to-all-done.1.refs_0_ = s16[8,528,256]{2,1,0:T(8,128)(2,1)S(1)} async-done(((s16[8,528,256]{2,1,0:T(8,128)(2,1)}), s16[8,528,256]{2,1,0:T(8,128)(2,1)S(1)}, u32[]{:S(2)}, u32[]{:S(2)}) %all-to-all-start.1) | async-done | bytes 2162720 | tf_op jit(solution)/shard_map/all_to_all | solution.py:438
  135.4 0.0 copy-start.1
  135.4 0.8 broadcast_in_dim.18.refs_2_
  136.1 0.7 copy-done.1
  136.8 17.3 %filter.1 = s16[8,528,256]{2,1,0:T(8,128)(2,1)} custom-call(s16[8,528,256]{2,1,0:T(8,128)(2,1)} %copy-done.1, f32[2,8,256,256]{3,2,1,0:T(8,128)} %pad_maximum_fusion.refs_1_, f32[2,8,16,256]{3,2,1,0:T(8,128)} %broadcast_in_dim.18.refs_2_, bf16[512,512]{1,0:T(8,128)(2,1)} %constant.116.clone.fh_ref.refs_3_.refs_2_, ...), custom_call_target="tpu_custom_call" | custom-call | tf_op jit(solution)/shard_map/filter/pallas_call | solution.py:401
  154.1 3.8 all-to-all-start.2
  157.9 0.0 copy-done
  158.0 0.7 fusion.10.refs_7_
  158.7 1.1 compare_convert_fusion.refs_6_
  159.8 25.2 %all-to-all-done.2.refs_0_ = s16[8,528,256]{2,1,0:T(8,128)(2,1)S(1)} async-done(((s16[8,528,256]{2,1,0:T(8,128)(2,1)}), s16[8,528,256]{2,1,0:T(8,128)(2,1)S(1)}, u32[]{:S(2)}, u32[]{:S(2)}) %all-to-all-start.2) | async-done | bytes 2162720 | tf_op jit(solution)/shard_map/all_to_all | solution.py:438
  185.0 0.0 copy-start.2
  185.0 1.4 copy-done.2
  186.4 18.1 %focus.1 = s16[8,528,256]{2,1,0:T(8,128)(2,1)} custom-call(s16[8,528,256]{2,1,0:T(8,128)(2,1)} %copy-done.2, f32[2,8,256,128]{3,2,1,0:T(8,128)} %broadcast_in_dim.15.tw_ref.refs_1_, bf16[512,512]{1,0:T(8,128)(2,1)} %constant.116.clone.fh_ref.refs_3_.refs_2_, bf16[512,512]{1,0:T(8,128)(2,1)} %constant.117.clone.fl_ref.refs_4_.refs_3_, ...), custom_call_target="tpu_custom_call" | custom-call | tf_op jit(solution)/shard_map/focus/pallas_call | solution.py:401
  204.5 31.6 %all_to_all.31.refs_0_ = s16[8,528,256]{2,1,0:T(8,128)(2,1)} all-to-all(s16[8,528,256]{2,1,0:T(8,128)(2,1)} %focus.1), channel_id=1, replica_groups=mesh['wave'=4,'zed'=4,'duo'=2] {'wave','duo'}, dimensions={0} | all-to-all | bytes 4325376 | tf_op jit(solution)/shard_map/all_to_all | solution.py:438
  236.1 17.3 %filter_back.1 = s16[8,528,256]{2,1,0:T(8,128)(2,1)} custom-call(s16[8,528,256]{2,1,0:T(8,128)(2,1)} %all_to_all.31.refs_0_, f32[2,8,256,256]{3,2,1,0:T(8,128)} %pad_maximum_fusion.refs_1_, f32[2,8,16,256]{3,2,1,0:T(8,128)} %broadcast_in_dim.18.refs_2_, bf16[512,512]{1,0:T(8,128)(2,1)} %constant.116.clone.fh_ref.refs_3_.refs_2_, ...), custom_call_target="tpu_custom_call" | custom-call | tf_op jit(solution)/shard_map/filter_back/pallas_call | solution.py:401
  253.4 31.6 %all_to_all.32.in_ref = s16[8,528,256]{2,1,0:T(8,128)(2,1)} all-to-all(s16[8,528,256]{2,1,0:T(8,128)(2,1)} %filter_back.1), channel_id=1, replica_groups=mesh['wave'=4,'zed'=4,'duo'=2] {'wave','duo'}, dimensions={0} | all-to-all | bytes 4325376 | tf_op jit(solution)/shard_map/all_to_all | solution.py:438
  285.1 9.6 %last.1 = bf16[8,2,256,256]{3,2,1,0:T(8,128)(2,1)} custom-call(s16[8,528,256]{2,1,0:T(8,128)(2,1)} %all_to_all.32.in_ref, f32[2,8,256,128]{3,2,1,0:T(8,128)} %broadcast_in_dim.15.tw_ref.refs_1_, bf16[512,512]{1,0:T(8,128)(2,1)} %constant.118.clone.refs_5_.refs_4_.gh_ref, bf16[512,512]{1,0:T(8,128)(2,1)} %constant.119.clone.refs_6_.refs_5_.gl_ref), custom_call_target="tpu_custom_call" | custom-call | tf_op jit(solution)/shard_map/last/pallas_call | solution.py:401
  294.7 3.6 all-to-all-start.5
  298.3 0.6 pad_maximum_fusion.1.back_w_ref
  298.9 48.4 %all-to-all-done.5 = bf16[8,2,256,256]{3,2,1,0:T(8,128)(2,1)S(1)} async-done(((bf16[8,2,256,256]{3,2,1,0:T(8,128)(2,1)}), bf16[8,2,256,256]{3,2,1,0:T(8,128)(2,1)S(1)}, u32[]{:S(2)}, u32[]{:S(2)}) %all-to-all-start.5) | async-done | bytes 2097184 | tf_op jit(solution)/shard_map/all_to_all | solution.py:438
  347.3 0.0 copy-start.3
  347.3 1.3 copy-done.3
  348.6 43.0 %width_slope.1 = f32[256,512]{1,0:T(8,128)} custom-call(s32[256,512]{1,0:T(8,128)} %levels_ref.3, f32[256,512]{1,0:T(8,128)} %offsets_ref.3, f32[256,256]{1,0:T(8,128)} %broadcast_in_dim.12.slope_ref, f32[256,256]{1,0:T(8,128)} %broadcast_in_dim.13.bias_ref, bf16[16,256]{1,0:T(8,128)(2,1)} %pad_maximum_fusion.1.back_w_ref, bf16[4,2,2,256,256]{4,3,2,1,0:T(8,128)(2,1)} %bitcast.14), custom_call_target="tpu_custom_call" | custom-call | tf_op jit(solution)/shard_map/width_slope/pallas_call | solution.py:210
  (9 shorter events, 0.1 us)
Async XLA Ops:
  0.0 157.9 %copy-start = (s32[4,64,2]{1,2,0:T(2,128)S(1)}, s32[4,64,2]{1,2,0:T(2,128)}, u32[]{:S(2)}) copy-start(s32[4,64,2]{1,2,0:T(2,128)} %param.16) | copy-start | bytes 6148
  35.5 55.6 %copy-start.4 = (f32[2,8,256]{2,1,0:T(8,128)S(1)}, f32[2,8,256]{2,1,0:T(8,128)}, u32[]{:S(2)}) copy-start(f32[2,8,256]{2,1,0:T(8,128)} %constant.120.clone) | copy-start | bytes 49156
  104.3 31.1 %all-to-all-start.1 = ((s16[8,528,256]{2,1,0:T(8,128)(2,1)}), s16[8,528,256]{2,1,0:T(8,128)(2,1)S(1)}, u32[]{:S(2)}, u32[]{:S(2)}) async-start(s16[8,528,256]{2,1,0:T(8,128)(2,1)} %first.1), calls=%async_computation.1 | async-start | bytes 4325376 | tf_op jit(solution)/shard_map/all_to_all | solution.py:438
  135.4 1.4 copy-start.1
  154.1 30.9 %all-to-all-start.2 = ((s16[8,528,256]{2,1,0:T(8,128)(2,1)}), s16[8,528,256]{2,1,0:T(8,128)(2,1)S(1)}, u32[]{:S(2)}, u32[]{:S(2)}) async-start(s16[8,528,256]{2,1,0:T(8,128)(2,1)} %filter.1), calls=%async_computation.2 | async-start | bytes 4325376 | tf_op jit(solution)/shard_map/all_to_all | solution.py:438
  185.0 1.4 copy-start.2
  294.7 52.6 %all-to-all-start.5 = ((bf16[8,2,256,256]{3,2,1,0:T(8,128)(2,1)}), bf16[8,2,256,256]{3,2,1,0:T(8,128)(2,1)S(1)}, u32[]{:S(2)}, u32[]{:S(2)}) async-start(bf16[8,2,256,256]{3,2,1,0:T(8,128)(2,1)} %last.1), calls=%async_computation.5 | async-start | bytes 4194304 | tf_op jit(solution)/shard_map/all_to_all | solution.py:438
  347.3 1.3 copy-start.3

commit v2 on v1

--- a/solution.py
+++ b/solution.py
@@ -114,116 +114,195 @@
     return x.astype(jnp.int32).astype(jnp.float32) if x.dtype == jnp.int16 else x
 
 
-def width_of(levels_ref, offsets_ref):
-    return 0.3 + levels_ref[...].astype(jnp.float32) * (0.4 / (LEVELS - 1)) + offsets_ref[...]
-
-
-def surrogate_kernel(levels_ref, offsets_ref, slope_ref, bias_ref, out_w_ref, out_b_ref, t_ref, width_s, mix_s):
-    waves, duo, parts, rows, cols = t_ref.shape
-    width_s[...] = width_of(levels_ref, offsets_ref)
-    units = slope_ref.shape[0]
-    lane = slope_ref.shape[1]
-    count = width_s.shape[1] // lane
-    for r in range(rows):
-        for c in range(count):
-            w = jnp.broadcast_to(width_s[r : r + 1, c * lane : (c + 1) * lane], (units, lane))
-            y = w * slope_ref[...] + bias_ref[...]
-            hidden = (y * jnp.tanh(y) + y).astype(jnp.bfloat16)
-            mixed = dot(out_w_ref[...], hidden)[: waves * parts] + out_b_ref[...]
-            mix_s[:, r, c * lane : (c + 1) * lane] = mixed
-    for wave in range(waves):
-        for d in range(duo):
-            for part in range(parts):
-                t_ref[wave, d, part] = mix_s[wave * parts + part, :, d * cols : (d + 1) * cols].astype(jnp.bfloat16)
-
-
-def slope_kernel(levels_ref, offsets_ref, slope_ref, bias_ref, back_w_ref, cot_ref, grad_ref, width_s, mix_s):
-    waves, duo, parts, rows, cols = cot_ref.shape
-    width_s[...] = width_of(levels_ref, offsets_ref)
-    units = slope_ref.shape[0]
-    lane = slope_ref.shape[1]
-    count = width_s.shape[1] // lane
-    js = waves * parts
-    for r in range(rows):
-        for c in range(count):
-            w = jnp.broadcast_to(width_s[r : r + 1, c * lane : (c + 1) * lane], (units, lane))
-            y = w * slope_ref[...] + bias_ref[...]
+class Exchange:
+    def __init__(self, axes, count, duo, send_sem, recv_sem, own_sem):
+        self.axes, self.count, self.duo = axes, count, duo
+        self.send_sem, self.recv_sem, self.own_sem = send_sem, recv_sem, own_sem
+        self.me = lax.axis_index(axes[0]) * duo + lax.axis_index(axes[1])
+
+    def other(self, step):
+        return lax.rem(self.me + step, self.count)
+
+    def device(self, index):
+        return {self.axes[0]: index // self.duo, self.axes[1]: lax.rem(index, self.duo)}
+
+    def enter(self):
+        barrier = pltpu.get_barrier_semaphore()
+        for step in range(1, self.count):
+            pl.semaphore_signal(
+                barrier, inc=1, device_id=self.device(self.other(step)), device_id_type=pl.DeviceIdType.MESH
+            )
+        pl.semaphore_wait(barrier, self.count - 1)
+
+    def copy(self, source, target, step, piece):
+        return pltpu.make_async_remote_copy(
+            src_ref=source,
+            dst_ref=target,
+            send_sem=self.send_sem.at[piece, step],
+            recv_sem=self.recv_sem.at[piece, step],
+            device_id=self.device(self.other(step)),
+            device_id_type=pl.DeviceIdType.MESH,
+        )
+
+    def own(self, source, target, piece):
+        return pltpu.make_async_copy(source, target, self.own_sem.at[piece])
+
+
+def exchange_scratch(count, pieces):
+    return [
+        pltpu.SemaphoreType.DMA((pieces, count)),
+        pltpu.SemaphoreType.DMA((pieces, count)),
+        pltpu.SemaphoreType.DMA((pieces,)),
+    ]
+
+
+PIECES = 4
+
+
+def send_piece(ex, send_s, out_ref, piece, rows, start):
+    at = pl.ds(piece * rows, rows)
+    for step in range(1, ex.count):
+        copy = ex.copy(send_s.at[ex.other(step), :, at, :], out_ref.at[ex.me, :, at, :], step, piece)
+        copy.start() if start else copy.wait()
+    copy = ex.own(send_s.at[ex.me, :, at, :], out_ref.at[ex.me, :, at, :], piece)
+    copy.start() if start else copy.wait()
+
+
+def blocks_out(ex, send_s, out_ref, fill, beside):
+    if ex is None:
+        def plain(k, _):
+            fill(k)
+            return 0
+
+        lax.fori_loop(0, RADIX, plain, 0)
+        beside()
+        return
+
+    def step_out(step, _):
+        k = ex.other(step)
+        fill(k)
+        ex.copy(send_s.at[k], out_ref.at[ex.me], step, 0).start()
+        return 0
+
+    lax.fori_loop(1, ex.count, step_out, 0)
+    fill(ex.me)
+    ex.own(send_s.at[ex.me], out_ref.at[ex.me], 0).start()
+    beside()
+    ex.own(send_s.at[ex.me], out_ref.at[ex.me], 0).wait()
+
+    def step_wait(step, _):
+        ex.copy(send_s.at[ex.other(step)], out_ref.at[ex.me], step, 0).wait()
+        return 0
+
+    lax.fori_loop(1, ex.count, step_wait, 0)
+
+
+def strip_widths(levels_ref, offsets_ref, row):
+    at = pl.ds(row, ROWS)
+    return 0.3 + levels_ref[at, :].astype(jnp.float32) * (0.4 / (LEVELS - 1)) + offsets_ref[at, :]
+
+
+def each_chunk(widths, slope_ref, bias_ref, body):
+    units, lane = slope_ref.shape
+    for r in range(ROWS):
+        for c in range(widths.shape[1] // lane):
+            lanes = slice(c * lane, (c + 1) * lane)
+            w = jnp.broadcast_to(widths[r : r + 1, lanes], (units, lane))
+            body(r, lanes, w * slope_ref[...] + bias_ref[...])
+
+
+def mixed_strips(levels_ref, offsets_ref, slope_ref, bias_ref, back_w_ref, mixed_ref, strip_s, first):
+    js = mixed_ref.shape[0]
+
+    def strip(i, _):
+        widths = strip_widths(levels_ref, offsets_ref, pl.multiple_of((first + i) * ROWS, ROWS))
+
+        def body(r, lanes, y):
             th = jnp.tanh(y)
             act = ((1.0 + th) * (1.0 + (y - y * th))).astype(jnp.bfloat16)
             mixed = dot(back_w_ref[...], act)
-            mix_s[:, r, c * lane : (c + 1) * lane] = mixed[:js] + mixed[js : 2 * js]
-    for d in range(duo):
-        at = slice(d * cols, (d + 1) * cols)
-        total = jnp.zeros((rows, cols), jnp.float32)
-        for wave in range(waves):
+            strip_s[:, r, lanes] = mixed[:js] + mixed[js : 2 * js]
+
+        each_chunk(widths, slope_ref, bias_ref, body)
+        mixed_ref[:, pl.ds(pl.multiple_of(i * ROWS, ROWS), ROWS), :] = strip_s[...]
+        return 0
+
+    lax.fori_loop(0, mixed_ref.shape[1] // ROWS, strip, 0)
+
+
+def surrogate_kernel(
+    make, levels_ref, offsets_ref, slope_ref, bias_ref, back_w_ref, out_w_ref, out_b_ref, out_ref, mixed_ref, strip_s, send_s, *sems
+):
+    waves_duo, parts, rows, cols = send_s.shape
+    js = strip_s.shape[0]
+    duo = strip_s.shape[2] // cols
+    ex = make(*sems) if sems else None
+    if ex is not None:
+        ex.enter()
+
+    def strip(i, _):
+        row = pl.multiple_of(i * ROWS, ROWS)
+        widths = strip_widths(levels_ref, offsets_ref, row)
+
+        def body(r, lanes, y):
+            hidden = (y * jnp.tanh(y) + y).astype(jnp.bfloat16)
+            strip_s[:, r, lanes] = dot(out_w_ref[...], hidden)[:js] + out_b_ref[...]
+
+        each_chunk(widths, slope_ref, bias_ref, body)
+        for block in range(waves_duo):
+            wave, d = block // duo, block % duo
             for part in range(parts):
-                total = total + mix_s[wave * parts + part, :, at] * cot_ref[wave, d, part].astype(jnp.float32)
-        grad_ref[:, at] = total
-
-
-def unit_tables(w_in, b_in, lane):
-    units = w_in.shape[0]
+                piece = strip_s[wave * parts + part, :, d * cols : (d + 1) * cols].astype(jnp.bfloat16)
+                send_s[block, part, pl.ds(row, ROWS), :] = piece
+        return 0
+
+    strips = rows // ROWS
+    if ex is None:
+        lax.fori_loop(0, strips, strip, 0)
+        out_ref[...] = send_s[...]
+    else:
+        for piece in range(PIECES):
+            lax.fori_loop(piece * strips // PIECES, (piece + 1) * strips // PIECES, strip, 0)
+            send_piece(ex, send_s, out_ref, piece, rows // PIECES, True)
+    mixed_strips(levels_ref, offsets_ref, slope_ref, bias_ref, back_w_ref, mixed_ref, strip_s, 0)
+    if ex is not None:
+        for piece in range(PIECES):
+            send_piece(ex, send_s, out_ref, piece, rows // PIECES, False)
+
+
+def gradient_kernel(*refs):
+    mixed_refs, cot_ref, grad_ref = refs[:-2], refs[-2], refs[-1]
+    blocks, parts, rows, cols = cot_ref.shape
+    duo = grad_ref.shape[1] // cols
+    base = 0
+    for mixed_ref in mixed_refs:
+        here = mixed_ref.shape[1]
+
+        def strip(i, _, mixed_ref=mixed_ref, base=base):
+            own = pl.ds(pl.multiple_of(i * ROWS, ROWS), ROWS)
+            at = pl.ds(pl.multiple_of(base + i * ROWS, ROWS), ROWS)
+            for d in range(duo):
+                lanes = slice(d * cols, (d + 1) * cols)
+                total = jnp.zeros((ROWS, cols), jnp.float32)
+                for block in range(d, blocks, duo):
+                    for part in range(parts):
+                        j = block // duo * parts + part
+                        total = total + mixed_ref[j, own, lanes] * cot_ref[block, part, at, :].astype(jnp.float32)
+                grad_ref[at, lanes] = total
+            return 0
+
+        lax.fori_loop(0, here // ROWS, strip, 0)
+        base += here
+
+
+def unit_tables(w_in, b_in, w_out, b_out, waves, lane):
+    units, js = w_out.shape
     spread = lambda x: jnp.broadcast_to((0.5 * x)[:, None], (units, lane))
-    return spread(w_in), spread(b_in)
-
-
-def whole(shape):
-    return pl.BlockSpec(shape, lambda i: (0,) * len(shape))
-
-
-def surrogate(levels, offsets, w_in, b_in, w_out, b_out, waves, duo):
-    rows, cols = levels.shape
-    parts = 2
-    js = waves * parts
-    units = w_in.shape[0]
-    lane = min(256, cols)
-    slope, bias = unit_tables(w_in, b_in, lane)
-    ordered = w_out.reshape(units, parts, waves).transpose(2, 1, 0).reshape(js, units)
-    pad = max(16, js)
-    ordered = jnp.zeros((pad, units), jnp.bfloat16).at[:js].set(ordered)
-    biases = b_out.reshape(parts, waves).T.reshape(js, 1)
-    shape = (waves, duo, parts, rows, cols // duo)
-    strip = pl.BlockSpec((ROWS, cols), lambda i: (i, 0))
-    return pl.pallas_call(
-        surrogate_kernel,
-        grid=(rows // ROWS,),
-        in_specs=[strip, strip, whole(slope.shape), whole(bias.shape), whole(ordered.shape), whole(biases.shape)],
-        out_specs=pl.BlockSpec(shape[:3] + (ROWS, cols // duo), lambda i: (0, 0, 0, i, 0)),
-        out_shape=jax.ShapeDtypeStruct(shape, jnp.bfloat16),
-        scratch_shapes=[pltpu.VMEM((ROWS, cols), jnp.float32), pltpu.VMEM((js, ROWS, cols), jnp.float32)],
-        compiler_params=params(),
-        name="surrogate",
-    )(levels, offsets, slope, bias, ordered, biases)
-
-
-def width_slope(levels, offsets, w_in, b_in, w_out, cot):
-    rows, cols = levels.shape
-    waves, duo, parts = cot.shape[:3]
-    js = waves * parts
-    units = w_in.shape[0]
-    lane = min(256, cols)
-    slope, bias = unit_tables(w_in, b_in, lane)
-    ordered = w_out.astype(jnp.float32).reshape(units, parts, waves).transpose(2, 1, 0).reshape(js, units)
-    high, low = halves(ordered * (0.5 * w_in)[None, :])
-    weights = jnp.concatenate([high, low])
-    strip = pl.BlockSpec((ROWS, cols), lambda i: (i, 0))
-    return pl.pallas_call(
-        slope_kernel,
-        grid=(rows // ROWS,),
-        in_specs=[
-            strip,
-            strip,
-            whole(slope.shape),
-            whole(bias.shape),
-            whole(weights.shape),
-            pl.BlockSpec(cot.shape[:3] + (ROWS, cols // duo), lambda i: (0, 0, 0, i, 0)),
-        ],
-        out_specs=strip,
-        out_shape=jax.ShapeDtypeStruct((rows, cols), jnp.float32),
-        scratch_shapes=[pltpu.VMEM((ROWS, cols), jnp.float32), pltpu.VMEM((js, ROWS, cols), jnp.float32)],
-        compiler_params=params(),
-        name="width_slope",
-    )(levels, offsets, slope, bias, weights, cot)
+    ordered = w_out.reshape(units, 2, waves).transpose(2, 1, 0).reshape(js, units)
+    out_w = jnp.zeros((max(16, js), units), jnp.bfloat16).at[:js].set(ordered)
+    out_b = b_out.reshape(2, waves).T.reshape(js, 1)
+    high, low = halves(ordered.astype(jnp.float32) * (0.5 * w_in)[None, :])
+    return spread(w_in), spread(b_in), jnp.concatenate([high, low]), out_w, out_b
 
 
 def col_forward_chunks(load, tw_ref, hi_s, lo_s):
@@ -246,16 +325,13 @@
     lax.fori_loop(0, points // ROWS, chunk, 0)
 
 
-def col_forward_dots(fh_ref, fl_ref, hi_s, lo_s, out_ref):
-    points = hi_s.shape[1] // 2
-
-    def step(k, _):
+def col_forward_dots(fh_ref, fl_ref, hi_s, lo_s, out_ref, send_s, ex, beside):
+    def fill(k):
         high = hi_s[k]
         y = dot(fh_ref[...], high) + dot(fh_ref[...], lo_s[k]) + dot(fl_ref[...], high)
-        put_block(out_ref, k, y)
-        return 0
-
-    lax.fori_loop(0, RADIX, step, 0)
+        put_block(send_s, k, y)
+
+    blocks_out(ex, send_s, out_ref, fill, beside)
 
 
 def col_inverse_dots(in_ref, gh_ref, gl_ref, tw_ref, mid_s):
@@ -278,17 +354,30 @@
     lax.fori_loop(0, RADIX, step, 0)
 
 
-def first_kernel(t_ref, tw_ref, fh_ref, fl_ref, out_ref, hi_s, lo_s):
+def first_kernel(make, t_ref, tw_ref, fh_ref, fl_ref, out_ref, kern_ref, hi_s, lo_s, send_s, *sems):
+    ex = make(*sems) if sems else None
+    if ex is not None:
+        ex.enter()
+
     def load(n, at, lanes):
         return (t_ref[n, 0, at, lanes].astype(jnp.float32), t_ref[n, 1, at, lanes].astype(jnp.float32))
 
     col_forward_chunks(load, tw_ref, hi_s, lo_s)
-    col_forward_dots(fh_ref, fl_ref, hi_s, lo_s, out_ref)
-
-
-def focus_kernel(level, waves, in_ref, tw_ref, fh_ref, fl_ref, gh_ref, gl_ref, rowsel_ref, colsel_ref, out_ref, hi_s, lo_s, mid_s, spot_s):
+    col_forward_dots(fh_ref, fl_ref, hi_s, lo_s, out_ref, send_s, ex, lambda: transfer_rows(kern_ref))
+    if ex is None:
+        out_ref[...] = send_s[...]
+
+
+def focus_kernel(
+    make, level, waves, first, in_ref, tw_ref, fh_ref, fl_ref, gh_ref, gl_ref, rowsel_ref, colsel_ref,
+    levels_ref, offsets_ref, slope_ref, bias_ref, back_w_ref,
+    out_ref, mixed_ref, hi_s, lo_s, mid_s, spot_s, strip_s, send_s, *sems
+):
     points, cols = mid_s.shape[2], mid_s.shape[3]
     lane = tw_ref.shape[3]
+    ex = make(*sems) if sems else None
+    if ex is not None:
+        ex.enter()
     col_inverse_dots(in_ref, gh_ref, gl_ref, tw_ref, mid_s)
     for n in range(RADIX):
         spot_s[n] = dot(rowsel_ref[n], colsel_ref[...]) * level
@@ -311,11 +400,20 @@
         return (mid_s[n, 0, at, lanes], mid_s[n, 1, at, lanes])
 
     col_forward_chunks(load, tw_ref, hi_s, lo_s)
-    col_forward_dots(fh_ref, fl_ref, hi_s, lo_s, out_ref)
-
-
-def last_kernel(in_ref, tw_ref, gh_ref, gl_ref, out_ref, mid_s):
+
+    def beside():
+        mixed_strips(levels_ref, offsets_ref, slope_ref, bias_ref, back_w_ref, mixed_ref, strip_s, first)
+
+    col_forward_dots(fh_ref, fl_ref, hi_s, lo_s, out_ref, send_s, ex, beside)
+    if ex is None:
+        out_ref[...] = send_s[...]
+
+
+def last_kernel(make, in_ref, tw_ref, gh_ref, gl_ref, out_ref, mid_s, send_s, *sems):
     points, cols = mid_s.shape[2], mid_s.shape[3]
+    ex = make(*sems) if sems else None
+    if ex is not None:
+        ex.enter()
     lane = tw_ref.shape[3]
     col_inverse_dots(in_ref, gh_ref, gl_ref, tw_ref, mid_s)
 
@@ -325,14 +423,30 @@
             lanes = slice(c * lane, (c + 1) * lane)
             out = dft8([(mid_s[k, 0, at, lanes], mid_s[k, 1, at, lanes]) for k in range(RADIX)], 1)
             for n in range(RADIX):
-                out_ref[n, 0, at, lanes] = out[n][0].astype(jnp.bfloat16)
-                out_ref[n, 1, at, lanes] = out[n][1].astype(jnp.bfloat16)
-        return 0
-
-    lax.fori_loop(0, points // ROWS, chunk, 0)
-
-
-def filter_kernel(conjugate, in_ref, kern_ref, tw_ref, fh_ref, fl_ref, gh_ref, gl_ref, out_ref, hi_s, lo_s, mid_s, sent_s):
+                send_s[n, 0, at, lanes] = out[n][0].astype(jnp.bfloat16)
+                send_s[n, 1, at, lanes] = out[n][1].astype(jnp.bfloat16)
+        return 0
+
+    chunks = points // ROWS
+    if ex is None:
+        lax.fori_loop(0, chunks, chunk, 0)
+        out_ref[...] = send_s[...]
+        return
+    for piece in range(PIECES):
+        lax.fori_loop(piece * chunks // PIECES, (piece + 1) * chunks // PIECES, chunk, 0)
+        send_piece(ex, send_s, out_ref, piece, points // PIECES, True)
+    for piece in range(PIECES):
+        send_piece(ex, send_s, out_ref, piece, points // PIECES, False)
+
+
+def filter_kernel(
+    make, conjugate, first, in_ref, kern_ref, tw_ref, fh_ref, fl_ref, gh_ref, gl_ref,
+    levels_ref, offsets_ref, slope_ref, bias_ref, back_w_ref,
+    out_ref, mixed_ref, hi_s, lo_s, mid_s, sent_s, strip_s, send_s, *sems
+):
+    ex = make(*sems) if sems else None
+    if ex is not None:
+        ex.enter()
     rows, points = mid_s.shape[2], mid_s.shape[3]
     lane = 128
     scale = 1.0 / (RADIX * points)
@@ -390,19 +504,31 @@
 
     lax.fori_loop(0, rows // ROWS, inverse, 0)
 
-    def send(n, _):
-        put_block(out_ref, n, mid_s[n].reshape(2 * rows, points))
-        return 0
-
-    lax.fori_loop(0, RADIX, send, 0)
-
-
-def call(kernel, out_shape, out_type, scratch, name, *args):
+    def beside():
+        mixed_strips(levels_ref, offsets_ref, slope_ref, bias_ref, back_w_ref, mixed_ref, strip_s, first)
+
+    blocks_out(ex, send_s, out_ref, lambda n: put_block(send_s, n, mid_s[n].reshape(2 * rows, points)), beside)
+    if ex is None:
+        out_ref[...] = send_s[...]
+
+
+def call(kernel, out_shapes, scratch, name, remote, *args):
+    specs = [pl.BlockSpec(memory_space=pltpu.VMEM) for _ in out_shapes]
+    more = {}
+    make = None
+    if remote is not None:
+        axes, count, duo, pieces, collective = remote
+        specs[0] = pl.BlockSpec(memory_space=pl.ANY)
+        scratch = scratch + exchange_scratch(count, pieces)
+        more = dict(collective_id=collective, has_side_effects=True)
+        make = lambda *sems: Exchange(axes, count, duo, *sems)
     return pl.pallas_call(
-        kernel,
-        out_shape=jax.ShapeDtypeStruct(out_shape, out_type),
+        lambda *refs: kernel(make, *refs),
+        in_specs=[pl.BlockSpec(memory_space=pltpu.VMEM)] * len(args),
+        out_specs=specs,
+        out_shape=out_shapes,
         scratch_shapes=scratch,
-        compiler_params=params(),
+        compiler_params=params(**more),
         name=name,
     )(*args)
 
@@ -412,14 +538,34 @@
     return signed_index.astype(jnp.float32) * (2.0 * math.pi / total_len)
 
 
-def transfer(wavelength, kx, ky, focal_length):
-    wave_number = 2.0 * math.pi / wavelength
-    kz_square = wave_number * wave_number - kx**2 - ky**2
-    kz_root = jnp.sqrt(jnp.abs(kz_square))
-    is_open = kz_square > 0.0
-    phase_angle = jnp.where(is_open, focal_length * kz_root, 0.0)
-    amplitude = jnp.where(is_open, 1.0, jnp.exp(-focal_length * kz_root))
-    return jnp.stack([amplitude * jnp.cos(phase_angle), amplitude * jnp.sin(phase_angle)])
+def transfer_rows(kern_ref):
+    rows, points = kern_ref.shape[2], kern_ref.shape[3]
+    length = RADIX * points
+    focal_length = float(length // 16)
+    waves, duo = lax.axis_size("wave"), lax.axis_size("duo")
+    own = lax.axis_index("wave") * duo + lax.axis_index("duo")
+    wavelength = 1.5 + lax.axis_index("zed").astype(jnp.float32) / (waves - 1)
+    wave_number = 2.0 * math.pi / jnp.full((ROWS, 128), wavelength, jnp.float32)
+
+    def chunk(i, _):
+        position = own * rows + i * ROWS + lax.broadcasted_iota(jnp.int32, (ROWS, 128), 0)
+        kx = frequencies(position // points + RADIX * lax.rem(position, points), length)
+        rest = wave_number * wave_number - kx * kx
+        at = pl.ds(pl.multiple_of(i * ROWS, ROWS), ROWS)
+        for k in range(RADIX):
+            for c in range(points // 128):
+                v = k + RADIX * (c * 128 + lax.broadcasted_iota(jnp.int32, (ROWS, 128), 1))
+                ky = frequencies(v, length)
+                kz_square = rest - ky * ky
+                kz_root = jnp.sqrt(jnp.abs(kz_square))
+                is_open = kz_square > 0.0
+                phase_angle = jnp.where(is_open, focal_length * kz_root, 0.0)
+                amplitude = jnp.where(is_open, 1.0, jnp.exp(-focal_length * kz_root))
+                kern_ref[0, k, at, c * 128 : (c + 1) * 128] = amplitude * jnp.cos(phase_angle)
+                kern_ref[1, k, at, c * 128 : (c + 1) * 128] = amplitude * jnp.sin(phase_angle)
+        return 0
+
+    lax.fori_loop(0, rows // ROWS, chunk, 0)
 
 
 def local(levels, offsets, targets, w_in, b_in, w_out, b_out):
@@ -432,7 +578,6 @@
     rows = length // group
     own = lax.axis_index("wave") * duo + lax.axis_index("duo")
     wave_index = lax.axis_index("zed")
-    wavelength = 1.5 + wave_index.astype(jnp.float32) / (waves - 1)
 
     def exchange(x, axes):
         return lax.all_to_all(x, axes, split_axis=0, concat_axis=0, tiled=True)
@@ -456,13 +601,6 @@
     lane = min(128, cols)
     tw_col = jnp.broadcast_to(jnp.asarray(tw)[:, :, :, None], (2, RADIX, points, lane))
     tw_row = jnp.broadcast_to(jnp.asarray(tw)[:, :, None, :], (2, RADIX, ROWS, points))
-
-    position = own * rows + jnp.arange(rows, dtype=jnp.int32)
-    u = position // points + RADIX * (position % points)
-    v = jnp.arange(RADIX, dtype=jnp.int32)[:, None] + RADIX * jnp.arange(points, dtype=jnp.int32)[None, :]
-    kern = transfer(
-        wavelength, frequencies(u, length)[None, :, None], frequencies(v, length)[:, None, :], float(length // 16)
-    )
 
     own_targets = lax.dynamic_index_in_dim(targets, wave_index, 0, keepdims=False)
     rowsel = (jnp.arange(length, dtype=jnp.int32)[:, None] == own_targets[None, :, 0]).astype(jnp.bfloat16)
@@ -488,34 +626,73 @@
             return exchange(x, GROUP)
         return regroup(exchange(recolumn(x.reshape(row_shape), group), GROUP), RADIX).reshape(col_send)
 
-    def filtered(spectrum, conjugate):
-        done = call(
-            lambda *refs: filter_kernel(conjugate, *refs),
-            row_send,
-            wire,
-            row_pair + [pltpu.VMEM(row_shape, jnp.float32), pltpu.VMEM((RADIX, ROWS, points), jnp.float32)],
+    f32, bf16 = jnp.float32, jnp.bfloat16
+    strips = rows_here // ROWS
+    quarter = strips // 4
+    js = 2 * waves
+    lane_units = min(256, cols_here)
+    slope, bias, back_w, out_w, out_b = unit_tables(w_in, b_in, w_out, b_out, waves, lane_units)
+    unit_args = (levels, offsets, slope, bias, back_w)
+    strip_s = pltpu.VMEM((js, ROWS, cols_here), f32)
+
+    def mixed_shape(count):
+        return jax.ShapeDtypeStruct((js, count * ROWS, cols_here), f32)
+
+    def remote(axes, pieces, collective):
+        return (axes, group, duo, pieces, collective) if coded else None
+
+    slab_shape = (slabs, 2, rows_here, cols)
+    trans, mixed_a = call(
+        surrogate_kernel,
+        [jax.ShapeDtypeStruct(slab_shape, bf16), mixed_shape(quarter)],
+        [strip_s, pltpu.VMEM(slab_shape, bf16)],
+        "surrogate", remote(SLAB, PIECES, 0), *unit_args, out_w, out_b,
+    )
+    if not coded:
+        trans = exchange(trans, SLAB)
+
+    spectrum, kern = call(
+        first_kernel,
+        [jax.ShapeDtypeStruct(col_send, wire), jax.ShapeDtypeStruct((2, RADIX, rows, points), f32)],
+        col_pair + [pltpu.VMEM(col_send, wire)],
+        "first", remote(GROUP, 1, 1), regroup(trans, RADIX), tw_col, fh, fl,
+    )
+
+    def filtered(spectrum, conjugate, first, collective):
+        there = spectrum if coded else to_rows(spectrum)
+        done, mixed = call(
+            lambda make, *refs: filter_kernel(make, conjugate, first, *refs),
+            [jax.ShapeDtypeStruct(row_send, wire), mixed_shape(quarter)],
+            row_pair + [pltpu.VMEM(row_shape, f32), pltpu.VMEM((RADIX, ROWS, points), f32), strip_s, pltpu.VMEM(row_send, wire)],
             "filter_back" if conjugate else "filter",
-            to_rows(spectrum), kern, tw_row, fh, fl, gh, gl,
+            remote(GROUP, 1, collective),
+            there, kern, tw_row, fh, fl, gh, gl, *unit_args,
         )
-        return to_cols(done)
-
-    trans = surrogate(levels, offsets, w_in, b_in, w_out, b_out, waves, duo)
-    trans = exchange(trans.reshape((slabs,) + trans.shape[2:]), SLAB)
-    spectrum = call(first_kernel, col_send, wire, col_pair, "first", regroup(trans, RADIX), tw_col, fh, fl)
-    spectrum = filtered(spectrum, False)
-    spectrum = call(
-        lambda *refs: focus_kernel(float(length // 8), waves, *refs),
-        col_send,
-        wire,
-        col_pair + [pltpu.VMEM(col_shape, jnp.float32), pltpu.VMEM((RADIX, points, cols), jnp.float32)],
-        "focus",
-        spectrum, tw_col, fh, fl, gh, gl, rowsel, colsel,
+        return (done if coded else to_cols(done)), mixed
+
+    spectrum, mixed_b = filtered(spectrum, False, quarter, 2)
+    spectrum, mixed_c = call(
+        lambda make, *refs: focus_kernel(make, float(length // 8), waves, 2 * quarter, *refs),
+        [jax.ShapeDtypeStruct(col_send, wire), mixed_shape(quarter)],
+        col_pair
+        + [pltpu.VMEM(col_shape, f32), pltpu.VMEM((RADIX, points, cols), f32), strip_s, pltpu.VMEM(col_send, wire)],
+        "focus", remote(GROUP, 1, 3), spectrum, tw_col, fh, fl, gh, gl, rowsel, colsel, *unit_args,
     )
-    spectrum = filtered(spectrum, True)
-    mid = [pltpu.VMEM(col_shape, jnp.float32)]
-    cot = call(last_kernel, col_shape, jnp.bfloat16, mid, "last", spectrum, tw_col, gh, gl)
-    cot = exchange(regroup(cot, slabs), SLAB)
-    return width_slope(levels, offsets, w_in, b_in, w_out, cot.reshape((waves, duo) + cot.shape[1:]))
+    spectrum, mixed_d = filtered(spectrum, True, 3 * quarter, 4)
+    (cot,) = call(
+        last_kernel,
+        [jax.ShapeDtypeStruct(col_shape, bf16)],
+        [pltpu.VMEM(col_shape, f32), pltpu.VMEM(col_shape, bf16)],
+        "last", remote(SLAB, PIECES, 5), spectrum, tw_col, gh, gl,
+    )
+    if not coded:
+        cot = exchange(regroup(cot, slabs), SLAB)
+    return pl.pallas_call(
+        gradient_kernel,
+        out_shape=jax.ShapeDtypeStruct((rows_here, cols_here), f32),
+        compiler_params=params(),
+        name="gradient",
+    )(mixed_a, mixed_b, mixed_c, mixed_d, cot)
 
 
 def solution(mesh):

time: 392 us -> 293 us (0.75)
  Pallas kernels: 146 us -> 280 us
  blocking collectives: 119 us -> 0 us
  waiting for transfers between devices: 89.9 us -> 0 us
  starting transfers between devices: 11.2 us -> 0 us
  other arithmetic: 14.7 us -> 3.82 us
    pallas_call x7, Pallas kernels: 146 us -> 280 us  [the longest x6 276 us: call(): pl.pallas_call(lambda *refs: kernel(make, *refs), in_specs=[pl.BlockSpec(...]
    all_to_all x3 -> x0, blocking collectives: 119 us -> none  [exchange(): return lax.all_to_all(x, axes, split_axis=0, concat_axis=0, tiled=True)]
    all_to_all x3 -> x0, waiting for transfers between devices: 89.9 us -> none  [exchange(): return lax.all_to_all(x, axes, split_axis=0, concat_axis=0, tiled=True)]
    all_to_all x3 -> x0, starting transfers between devices: 11.2 us -> none  [exchange(): return lax.all_to_all(x, axes, split_axis=0, concat_axis=0, tiled=True)]
    mul x2 -> x0, other arithmetic: 8.45 us -> none  [the longest x1 8.45 us: transfer(): amplitude * jnp.cos(phase_angle)]
  transfers between devices with their start and end apart: 3 -> 0, of which waited for: 3 -> 0; matrix products, arithmetic and copies ran while one was open for 3% -> 0% of each run, Pallas kernels for 0% -> 0%
where the time goes in v2:
time: 293 us; the launch traced here: 291 us
  Pallas kernels  280 us (96%)
  local copies, waits for them, and re-layouts  7.19 us (2%)
  other arithmetic  3.82 us (1%)
    pallas_call x6, Pallas kernels, call(): pl.pallas_call(lambda *refs: kernel(make, *refs), in_specs=[pl.BlockSpec(...  276 us

profile of v2, /device:TPU:0, one launch (start us, length us, event | category | flops | bytes accessed | tf_op | source)
XLA Modules:
  0.0 291.1 jit_solution(15754620464209206352)
XLA Ops:
  0.0 0.0 copy-start
  0.0 0.0 copy-start.1
  0.0 0.7 broadcast_multiply_fusion.1
  0.7 0.8 broadcast_in_dim.8.refs_2_.refs_9_.refs_10_
  1.5 0.7 broadcast_multiply_fusion
  2.2 0.8 broadcast_in_dim.9.refs_3_.refs_10_.refs_11_
  3.0 0.7 reshape.59
  3.8 0.6 pad_maximum_fusion.refs_4_.refs_11_.refs_12_
  4.4 0.6 scatter.4.refs_5_
  5.0 0.7 reshape.61
  5.7 0.1 copy.17
  5.8 0.7 reshape.63.refs_6_
  6.5 57.3 %surrogate.1 = (bf16[8,2,256,256]{3,2,1,0:T(8,128)(2,1)}, f32[8,64,512]{2,1,0:T(8,128)}) custom-call(s32[256,512]{1,0:T(8,128)} %refs_7_.3, f32[256,512]{1,0:T(8,128)} %refs_8_.5, f32[256,256]{1,0:T(8,128)} %broadcast_in_dim.8.refs_2_.refs_9_.refs_10_, f32[256,256]{1,0:T(8,128)} %broadcast_in_dim.9.refs_3_.refs_10_.refs_11_, ...), custom_call_target="tpu_custom_call" | custom-call | tf_op jit(solution)/shard_map/surrogate/pallas_call | solution.py:525
  63.8 0.0 copy-done.1
  63.8 2.0 broadcast_in_dim.10.refs_1_
  65.8 34.2 %first.1 = (s16[8,528,256]{2,1,0:T(8,128)(2,1)}, f32[2,8,256,256]{3,2,1,0:T(8,128)}) custom-call(bf16[8,2,256,256]{3,2,1,0:T(8,128)(2,1)} %get-tuple-element.28.refs_0_, f32[2,8,256,128]{3,2,1,0:T(8,128)} %broadcast_in_dim.10.refs_1_, bf16[512,512]{1,0:T(8,128)(2,1)} %constant.62.clone.refs_2_.refs_3_, bf16[512,512]{1,0:T(8,128)(2,1)} %constant.63.clone.refs_3_.refs_4_), custom_call_target="tpu_custom_call" | custom-call | tf_op jit(solution)/shard_map/first/pallas_call | solution.py:525
  100.0 0.7 broadcast_in_dim.11.refs_2_
  100.7 43.7 %filter.1 = (s16[8,528,256]{2,1,0:T(8,128)(2,1)}, f32[8,64,512]{2,1,0:T(8,128)}) custom-call(s16[8,528,256]{2,1,0:T(8,128)(2,1)} %get-tuple-element.29.refs_0_, f32[2,8,256,256]{3,2,1,0:T(8,128)} %get-tuple-element.30.refs_1_, f32[2,8,16,256]{3,2,1,0:T(8,128)} %broadcast_in_dim.11.refs_2_, bf16[512,512]{1,0:T(8,128)(2,1)} %constant.62.clone.refs_2_.refs_3_, ...), custom_call_target="tpu_custom_call" | custom-call | tf_op jit(solution)/shard_map/filter/pallas_call | solution.py:525
  144.4 0.0 copy-done
  144.5 1.1 compare_convert_fusion.refs_6_
  145.6 0.7 fusion.refs_7_
  146.3 40.3 %focus.1 = (s16[8,528,256]{2,1,0:T(8,128)(2,1)}, f32[8,64,512]{2,1,0:T(8,128)}) custom-call(s16[8,528,256]{2,1,0:T(8,128)(2,1)} %get-tuple-element.32.refs_0_, f32[2,8,256,128]{3,2,1,0:T(8,128)} %broadcast_in_dim.10.refs_1_, bf16[512,512]{1,0:T(8,128)(2,1)} %constant.62.clone.refs_2_.refs_3_, bf16[512,512]{1,0:T(8,128)(2,1)} %constant.63.clone.refs_3_.refs_4_, ...), custom_call_target="tpu_custom_call" | custom-call | tf_op jit(solution)/shard_map/focus/pallas_call | solution.py:525
  186.6 43.7 %filter_back.1 = (s16[8,528,256]{2,1,0:T(8,128)(2,1)}, f32[8,64,512]{2,1,0:T(8,128)}) custom-call(s16[8,528,256]{2,1,0:T(8,128)(2,1)} %get-tuple-element.34.refs_0_, f32[2,8,256,256]{3,2,1,0:T(8,128)} %get-tuple-element.30.refs_1_, f32[2,8,16,256]{3,2,1,0:T(8,128)} %broadcast_in_dim.11.refs_2_, bf16[512,512]{1,0:T(8,128)(2,1)} %constant.62.clone.refs_2_.refs_3_, ...), custom_call_target="tpu_custom_call" | custom-call | tf_op jit(solution)/shard_map/filter_back/pallas_call | solution.py:525
  230.4 56.5 %last.1.refs_4_ = bf16[8,2,256,256]{3,2,1,0:T(8,128)(2,1)} custom-call(s16[8,528,256]{2,1,0:T(8,128)(2,1)} %get-tuple-element.36.refs_0_, f32[2,8,256,128]{3,2,1,0:T(8,128)} %broadcast_in_dim.10.refs_1_, bf16[512,512]{1,0:T(8,128)(2,1)} %constant.64.clone.refs_5_.refs_4_.refs_2_, bf16[512,512]{1,0:T(8,128)(2,1)} %constant.65.clone.refs_6_.refs_5_.refs_3_), custom_call_target="tpu_custom_call" | custom-call | tf_op jit(solution)/shard_map/last/pallas_call | solution.py:525
  286.8 4.2 %gradient.1 = f32[256,512]{1,0:T(8,128)} custom-call(f32[8,64,512]{2,1,0:T(8,128)} %get-tuple-element.27.refs_0_, f32[8,64,512]{2,1,0:T(8,128)} %get-tuple-element.31.refs_1_, f32[8,64,512]{2,1,0:T(8,128)} %get-tuple-element.33.refs_2_, f32[8,64,512]{2,1,0:T(8,128)} %get-tuple-element.35.refs_3_, bf16[8,2,256,256]{3,2,1,0:T(8,128)(2,1)} %last.1.refs_4_), custom_call_target="tpu_custom_call" | custom-call | tf_op jit(solution)/shard_map/gradient/pallas_call | solution.py:690
  (6 shorter events, 0.0 us)
Async XLA Ops:
  0.0 144.4 %copy-start = (s32[4,64,2]{1,2,0:T(2,128)S(1)}, s32[4,64,2]{1,2,0:T(2,128)}, u32[]{:S(2)}) copy-start(s32[4,64,2]{1,2,0:T(2,128)} %param.16) | copy-start | bytes 6148
  0.0 63.8 %copy-start.1 = (f32[2,8,256]{2,1,0:T(8,128)S(1)}, f32[2,8,256]{2,1,0:T(8,128)}, u32[]{:S(2)}) copy-start(f32[2,8,256]{2,1,0:T(8,128)} %constant.66.clone) | copy-start | bytes 49156
